TPU v7x, 256 devices: a whole 4x4x8 slice. The times are simulated.
256 devices in a mesh: az: 32 (over z_hi, y, x), rad: 8 (over z_lo, core).
Axes of the slice: x: 4, y: 4, z: 8 (z_hi: 2, z_lo: 4; z = z_hi * 4 + z_lo), core: 2. Of those that a mesh axis runs over, the one named last changes fastest.
Arguments:
- density: float32 [2, 2048, 16384], P(None, 'rad', 'az'), may hold values from 0.5 to 2
- mom_r: float32 [2, 2048, 16384], P(None, 'rad', 'az'), may hold values from -1 to 1
- mom_phi: float32 [2, 2048, 16384], P(None, 'rad', 'az'), may hold values from 0.5 to 1.5
- potential_kernel: bfloat16 [64, 2048, 2048], P('az', 'rad'), may hold values from -2 to 2
- force_kernel: bfloat16 [64, 2048, 2048], P('az', 'rad'), may hold values from -2 to 2
Outputs:
- new_density: float32 [2, 2048, 16384], P(None, 'rad', 'az')
- new_mom_r: float32 [2, 2048, 16384], P(None, 'rad', 'az')
- new_mom_phi: float32 [2, 2048, 16384], P(None, 'rad', 'az')
- potential: float32 [2048, 16384], P('rad', 'az')
All inputs are finite; a program needn't handle non-finite values.
Results may differ from a plain program's by a relative error of at most 0.0015.
The roundings to bfloat16 on the way count: a program that leaves them out, or rounds other values in their place, can miss the bound.
Values may be sent and summed in bfloat16 or wider, within the bound.
A program may use at most 128 MiB of HBM per device.

v0:
```python
import math

import jax
import jax.numpy as jnp
from jax import lax
from jax.sharding import PartitionSpec as P

NAZ = 16384
MODES = 64


aspect_sq = 0.0025


def in_blocks(shard, dim, size):
    before, after = (shard.shape[:dim], shard.shape[dim + 1 :])
    return jnp.moveaxis(shard.reshape(*before, size, -1, *after), dim, 0)


def sum_at_owner(shard, axis, dim):
    blocks = in_blocks(shard, dim, lax.axis_size(axis))
    arrived = lax.all_to_all(blocks, axis, split_axis=0, concat_axis=0, tiled=True)
    return arrived.sum(axis=0)


def laid_out(blocks, dim):
    lengths = list(blocks.shape[1:])
    lengths[dim] *= blocks.shape[0]
    return jnp.moveaxis(blocks, 0, dim).reshape(lengths)


def copy_for_each(shard, axis):
    size = lax.axis_size(axis)
    return lax.all_to_all(
        jnp.broadcast_to(shard[None], (size, *shard.shape)), axis, 0, 0, tiled=True
    )


def gathered_copies(shard, axis, dim):
    return laid_out(copy_for_each(shard, axis), dim)


def rows_first(arrays, axis, dims):
    turned = [jnp.moveaxis(a, dim, 0) for a, dim in zip(arrays, dims)]
    both = jnp.concatenate([t.reshape(len(t), -1) for t in turned], axis=1)
    result, at, gathered = (lax.all_gather(both, axis, axis=0, tiled=True), 0, [])
    for t, dim in zip(turned, dims):
        slab = result[:, at : at + t[0].size].reshape(-1, *t.shape[1:])
        gathered.append(jnp.moveaxis(slab, 0, dim))
        at += t[0].size
    return tuple(gathered)


def extended(block, sides, width, periodic):
    for axis, dim in sides:
        count = lax.axis_size(axis)
        forward = [(i, i + 1) for i in range(count - 1)]
        if periodic:
            forward.append((count - 1, 0))
        backward = [(target, source) for source, target in forward]
        low = lax.ppermute(
            lax.slice_in_dim(block, block.shape[dim] - width, None, axis=dim), axis, forward
        )
        high = lax.ppermute(lax.slice_in_dim(block, 0, width, axis=dim), axis, backward)
        block = jnp.concatenate([low, block, high], axis=dim)
    return block


def mode_table(azimuth):
    mode_index = jnp.arange(MODES).astype(jnp.float32)
    angles = azimuth[:, None] * mode_index[None, :]
    basis = jnp.stack([jnp.cos(angles), jnp.sin(angles)], axis=-1).reshape(
        azimuth.shape[0], 2 * MODES
    )
    slope = jnp.stack(
        [-mode_index * jnp.sin(angles), mode_index * jnp.cos(angles)], axis=-1
    ).reshape(azimuth.shape[0], 2 * MODES)
    return (basis, slope)


def radial_flux(lower_side, upper_side, sound):

    def physical(fields):
        velocity = fields[1] / fields[0]
        flux = jnp.stack(
            [fields[1], fields[1] * velocity + sound * fields[0], fields[2] * velocity]
        )
        return (flux, velocity)

    flux_lower, vel_lower = physical(lower_side)
    flux_upper, vel_upper = physical(upper_side)
    wave_speed = jnp.maximum(jnp.abs(vel_lower), jnp.abs(vel_upper)) + jnp.sqrt(sound)
    return 0.5 * (flux_lower + flux_upper) - 0.5 * wave_speed * (upper_side - lower_side)


def azimuth_flux(lower_side, upper_side, sound):

    def physical(fields):
        velocity = fields[2] / fields[0]
        flux = jnp.stack(
            [fields[2], fields[1] * velocity, fields[2] * velocity + sound * fields[0]]
        )
        return (flux, velocity)

    flux_lower, vel_lower = physical(lower_side)
    flux_upper, vel_upper = physical(upper_side)
    wave_speed = jnp.maximum(jnp.abs(vel_lower), jnp.abs(vel_upper)) + jnp.sqrt(sound)
    return 0.5 * (flux_lower + flux_upper) - 0.5 * wave_speed * (upper_side - lower_side)


def tendency(fields, radial_ext, azimuth_ext, face_radius, grav_radial, grav_azimuth, cell_step):
    inner_radius = face_radius[:-1]
    outer_radius = face_radius[1:]
    mid_radius = 0.5 * (inner_radius + outer_radius)
    cell_area = 0.5 * (outer_radius * outer_radius - inner_radius * inner_radius)
    sound_face = (aspect_sq / face_radius)[:, None]
    sound_mid = (aspect_sq / mid_radius)[:, None]
    flux_rad = radial_flux(radial_ext[:, :, :-1], radial_ext[:, :, 1:], sound_face)
    flux_azi = azimuth_flux(azimuth_ext[..., :-1], azimuth_ext[..., 1:], sound_mid)
    weighted = flux_rad * face_radius[:, None]
    divergence = (weighted[:, :, 1:] - weighted[:, :, :-1]) / cell_area[:, None]
    divergence = divergence + (flux_azi[..., 1:] - flux_azi[..., :-1]) / (
        mid_radius[:, None] * cell_step
    )
    surface_now = fields[0]
    radial_mom = fields[1]
    spin_mom = fields[2]
    centre = mid_radius[:, None]
    source_rad = (spin_mom * spin_mom / surface_now + sound_mid * surface_now) / centre
    source_rad = source_rad + surface_now * (grav_radial / cell_step - 1.0 / (centre * centre))
    source_azi = -radial_mom * spin_mom / (surface_now * centre) + surface_now * (
        grav_azimuth / cell_step
    )
    source = jnp.stack([jnp.zeros_like(surface_now), source_rad, source_azi])
    return fields + 0.1 * cell_step * (source - divergence)


def local(density, mom_r, mom_phi, potential_kernel, force_kernel):
    highest = lax.Precision.HIGHEST
    row_count = density.shape[1]
    cell_count = density.shape[2]
    mode_count = potential_kernel.shape[0]
    col_count = 2 * mode_count
    cell_step = 2.0 * math.pi / NAZ
    az_index = lax.axis_index("az")
    rad_index = lax.axis_index("rad")
    azimuth = (
        (az_index * cell_count + jnp.arange(cell_count)).astype(jnp.float32) + 0.5
    ) * cell_step
    basis, slope = mode_table(azimuth)
    surface = jnp.sum(density, axis=0)
    partial_modes = jnp.dot(surface, basis, precision=highest) / NAZ
    own_modes = sum_at_owner(partial_modes, "az", 1)
    own_pairs = own_modes.astype(jnp.bfloat16)
    portion = gathered_copies(own_pairs, "rad", 0)
    count = portion.shape[0]
    pairs = portion.reshape(count, mode_count, 2)
    pot_part = jnp.einsum(
        "krs,skc->rkc", potential_kernel, pairs, preferred_element_type=jnp.float32
    ).reshape(row_count, col_count)
    force_part = jnp.einsum(
        "krs,skc->rkc", force_kernel, pairs, preferred_element_type=jnp.float32
    ).reshape(row_count, col_count)
    basis_rows = basis.T
    slope_rows = slope.T
    portion = rows_first((pot_part, force_part), "az", (1, 1))
    potential = jnp.dot(portion[0], basis_rows, precision=highest)
    grav_radial = jnp.dot(portion[1], basis_rows, precision=highest)
    slope_sum = jnp.dot(portion[0], slope_rows, precision=highest)
    face_radius = jnp.exp(
        (rad_index * row_count + jnp.arange(row_count + 1)).astype(jnp.float32) * cell_step
    )
    mid_radius = 0.5 * (face_radius[:-1] + face_radius[1:])
    grav_azimuth = -slope_sum / mid_radius[:, None]
    fields = jnp.stack([density, mom_r, mom_phi])
    azimuth_ext = extended(fields.astype(jnp.bfloat16), (("az", 3),), 1, True).astype(fields.dtype)
    radial_halo = extended(fields.astype(jnp.bfloat16), (("rad", 2),), 1, False).astype(
        fields.dtype
    )
    inner_rim = jnp.where(rad_index == 0, fields[:, :, :1], radial_halo[:, :, :1])
    outer_rim = jnp.where(
        rad_index == lax.axis_size("rad") - 1, fields[:, :, -1:], radial_halo[:, :, -1:]
    )
    radial_ext = jnp.concatenate([inner_rim, fields, outer_rim], axis=2)
    result = tendency(
        fields, radial_ext, azimuth_ext, face_radius, grav_radial, grav_azimuth, cell_step
    )
    return (result[0], result[1], result[2], potential)


def solution(mesh):
    placed = (
        P(None, "rad", "az"),
        P(None, "rad", "az"),
        P(None, "rad", "az"),
        P("az", "rad", None),
        P("az", "rad", None),
    )
    return jax.shard_map(
        local,
        mesh=mesh,
        in_specs=placed,
        out_specs=(
            P(None, "rad", "az"),
            P(None, "rad", "az"),
            P(None, "rad", "az"),
            P("rad", "az"),
        ),
        check_vma=False,
    )
```

profile of v0, /device:TPU:32, one launch (start us, length us, event | category | flops | bytes accessed | tf_op | source)
XLA Modules:
  0.0 215.3 jit_solution(8879129993631499688)
XLA Ops:
  0.6 2.3 %fusion.22 = bf16[3,2,256,512]{3,2,1,0:T(8,128)(2,1)S(1)} fusion(f32[1,2,256,512]{3,2,1,0:T(8,128)} %bitcast.53, f32[1,2,256,512]{3,2,1,0:T(8,128)} %bitcast.58, f32[1,2,256,512]{3,2,1,0:T(8,128)} %bitcast.48), kind=kLoop, calls=%fused_computation.76 | loop fusion | flops 1572864 | bytes 4718592 | tf_op jit(solution)/shard_map/convert_element_type | solution.py:177
  3.0 1.1 fusion.25
  4.1 10.9 %collective-permute-start.3 = (bf16[3,2,256,1]{3,2,1,0:T(8,128)(2,1)}, bf16[3,2,256,1]{3,2,1,0:T(8,128)(2,1)}, u32[]{:S(2)}, u32[]{:S(2)}) collective-permute-start(bf16[3,2,256,1]{3,2,1,0:T(8,128)(2,1)} %get-tuple-element.34), channel_id=1, source_target_pairs={{8,0},{16,8},{24,16},{32,24},{40,32},{48,40},{56,48},{64,56},{72,6... | collective-permute-start | bytes 9224 | tf_op jit(solution)/shard_map/ppermute | solution.py:64
  15.6 2.1 collective-permute-start.1
  17.7 2.3 %collective-permute-start = (bf16[3,2,1,512]{3,2,1,0:T(2,128)(2,1)}, bf16[3,2,1,512]{3,2,1,0:T(2,128)(2,1)}, u32[]{:S(2)}, u32[]{:S(2)}) collective-permute-start(bf16[3,2,1,512]{3,2,1,0:T(2,128)(2,1)} %get-tuple-element.31), channel_id=1, source_target_pairs={{0,1},{1,2},{2,3},{3,4},{4,5},{5,6},{6,7},{8,9},{9,10},{10,11},{11... | collective-permute-start | bytes 18440 | tf_op jit(solution)/shard_map/ppermute | solution.py:61
  20.6 0.8 pad_maximum_fusion.2
  21.3 0.9 copy.10
  22.2 1.1 reshape.288
  23.4 0.9 reduce_sum.18
  24.3 1.7 convolution_multiply_fusion.1
  26.7 11.8 %all-to-all-start = ((f32[32,256,4]{1,2,0:T(4,128)}), f32[32,256,4]{1,2,0:T(4,128)S(1)}, u32[]{:S(2)}, u32[]{:S(2)}) async-start(f32[32,256,4]{1,2,0:T(4,128)} %bitcast.63), calls=%async_computation | async-start | bytes 262144 | tf_op jit(solution)/shard_map/all_to_all | solution.py:22
  38.5 3.8 %pad_maximum_fusion.1 = f32[3,2,256,512]{3,2,1,0:T(8,128)} fusion(f32[1,2,256,512]{3,2,1,0:T(8,128)} %bitcast.54, f32[1,2,256,512]{3,2,1,0:T(8,128)} %bitcast.59, f32[1,2,256,512]{3,2,1,0:T(8,128)S(1)} %bitcast.49), kind=kLoop, calls=%fused_computation.19 | loop fusion | flops 1572864 | bytes 6291456 | tf_op jit(solution)/shard_map/stack | solution.py:175
  44.7 1.9 copy.12
  46.6 1.8 reshape.292
  49.0 2.5 %maximum_convert_fusion = f32[3,2,256,514]{3,2,1,0:T(8,128)S(1)} fusion(bf16[3,2,256,1]{3,2,1,0:T(8,128)(2,1)} %collective-permute-done.3, bf16[3,2,256,512]{3,2,1,0:T(8,128)(2,1)} %copy-done.8, bf16[3,2,256,1]{3,2,1,0:T(8,128)(2,1)} %collective-permute-done.2), kind=kLoop, calls=%fused_computation.20 | loop fusion | flops 4737024 | bytes 4737024 | tf_op jit(solution)/shard_map/convert_element_type | solution.py:176
  51.4 1.4 multiply_add_fusion
  52.9 2.5 %fusion.1 = f32[3,2,256,513]{3,2,1,0:T(8,128)} fusion(f32[3,2,256,514]{3,2,1,0:T(8,128)S(1)} %maximum_convert_fusion, f32[1,2,256,513]{3,2,1,0:T(8,128)S(1)} %get-tuple-element.11, f32[1,2,256,513]{3,2,1,0:T(8,128)S(1)} %get-tuple-element.15, f32[1,2,256,513]{3,2,1,0:T(8,128)S(1)} %get-tuple-element.16, f32[1,2,256,513]{3,2,1,0:T(8,128)S(1)} %get-tuple-element.10, ...), kind=kLoop, calls=%fused_computation.2 | loop fusion | flops 7091712 | bytes 16809984 | tf_op jit(solution)/shard_map/sub | solution.py:108
  56.0 1.0 broadcast_select_fusion
  57.1 0.8 pad_maximum_fusion
  58.0 4.3 %multiply_bitcast_fusion.1 = (f32[2,257,512]{2,1,0:T(8,128)}, f32[1,2,257,512]{3,2,1,0:T(8,128)}, f32[1,2,257,512]{3,2,1,0:T(8,128)}, f32[1,2,257,512]{3,2,1,0:T...) fusion(f32[257]{0:T(512)S(1)} %copy-done.17, ...), kind=kLoop, calls=%fused_computation.38 | loop fusion | flops 3947520 | bytes 13686792 | tf_op jit(solution)/shard_map/mul | solution.py:93
  62.9 1.3 broadcast_in_dim.2
  64.2 4.8 %all-to-all-start.1 = ((bf16[8,256,4]{1,2,0:T(4,128)(2,1)}), bf16[8,256,4]{1,2,0:T(4,128)(2,1)S(1)}, u32[]{:S(2)}, u32[]{:S(2)}) async-start(bf16[8,256,4]{1,2,0:T(4,128)(2,1)} %broadcast_in_dim.2), calls=%async_computation.1 | async-start | bytes 32768 | tf_op jit(solution)/shard_map/all_to_all | solution.py:34
  69.0 7.4 %fusion.5 = f32[3,2,257,512]{3,2,1,0:T(8,128)} fusion(f32[1,2,257,512]{3,2,1,0:T(8,128)} %get-tuple-element.22, f32[1,2,257,512]{3,2,1,0:T(8,128)} %get-tuple-element.19, f32[1,2,257,512]{3,2,1,0:T(8,128)} %get-tuple-element.23, f32[1,2,257,512]{3,2,1,0:T(8,128)} %get-tuple-element.20, f32[1,2,257,512]{3,2,1,0:T(8,128)} %get-tuple-element.18, ...), kind=kLoop, calls=%fused_computation.9 | loop fusion | flops 12632064 | bytes 13698052 | tf_op jit(solution)/shard_map/mul | solution.py:120
  77.2 2.2 %convolution_bitcast_fusion.1 = f32[256,2,2]{0,2,1:T(2,128)S(1)} fusion(bf16[2048,2,2]{0,2,1:T(2,128)(2,1)S(1)} %reshape_reshape.3, bf16[2,256,2048]{2,1,0:T(8,128)(2,1)} %param.8), kind=kOutput, calls=%fused_computation.35 | convolution fusion | flops 4194304 | bytes 2117632 | tf_op jit(solution)/shard_map/krs,skc->rkc/dot_general | solution.py:158
  79.4 122.8 %all-gather = f32[32,4,512]{2,1,0:T(4,128)} all-gather(f32[1,4,512]{2,1,0:T(4,128)S(1)} %maximum_bitcast_fusion), channel_id=1, replica_groups=mesh['az'=32,'rad'=8] {'az'}, dimensions={0}, use_global_device_ids=true | all-gather | bytes 270336 | tf_op jit(solution)/shard_map/all_gather | solution.py:46
  202.2 1.7 reshape.294
  203.9 2.5 %fusion.16 = f32[256,512]{1,0:T(8,128)} fusion(f32[512,128]{0,1:T(8,128)S(1)} %reshape.288, f32[128,512]{1,0:T(8,128)} %reshape.294), kind=kOutput, calls=%fused_computation.53 | convolution fusion | flops 201326592 | bytes 917504 | tf_op jit(solution)/shard_map/dot_general | solution.py:167
  206.4 1.5 fusion.14
  208.0 1.8 fusion.13
  210.6 1.3 copy-done.6
  211.8 1.7 fusion.10
  213.6 1.7 slice_bitcast_fusion
  (71 shorter events, 7.6 us)
Async XLA Ops:
  0.6 75.8 %copy-start = (bf16[2,256,2048]{2,1,0:T(8,128)(2,1)S(1)}, bf16[2,256,2048]{2,1,0:T(8,128)(2,1)}, u32[]{:S(2)}) copy-start(bf16[2,256,2048]{2,1,0:T(8,128)(2,1)} %param.9) | copy-start | bytes 6291460
  3.0 12.0 %copy-start.8 = (bf16[3,2,256,512]{3,2,1,0:T(8,128)(2,1)}, bf16[3,2,256,512]{3,2,1,0:T(8,128)(2,1)S(1)}, u32[]{:S(2)}) copy-start(bf16[3,2,256,512]{3,2,1,0:T(8,128)(2,1)S(1)} %fusion.22) | copy-start | bytes 4718596
  3.0 20.3 %copy-start.1 = (f32[2,256,512]{2,1,0:T(8,128)S(1)}, f32[2,256,512]{2,1,0:T(8,128)}, u32[]{:S(2)}) copy-start(f32[2,256,512]{2,1,0:T(8,128)} %param.5) | copy-start | bytes 3145732
  4.1 44.9 %collective-permute-start.3 = (bf16[3,2,256,1]{3,2,1,0:T(8,128)(2,1)}, bf16[3,2,256,1]{3,2,1,0:T(8,128)(2,1)}, u32[]{:S(2)}, u32[]{:S(2)}) collective-permute-start(bf16[3,2,256,1]{3,2,1,0:T(8,128)(2,1)} %get-tuple-element.34), channel_id=1, source_target_pairs={{8,0},{16,8},{24,16},{32,24},{40,32},{48,40},{56,48},{64,56},{72,6... | collective-permute-start | bytes 9224 | tf_op jit(solution)/shard_map/ppermute | solution.py:64
  15.0 33.9 %collective-permute-start.2 = (bf16[3,2,256,1]{3,2,1,0:T(8,128)(2,1)}, bf16[3,2,256,1]{3,2,1,0:T(8,128)(2,1)}, u32[]{:S(2)}, u32[]{:S(2)}) collective-permute-start(bf16[3,2,256,1]{3,2,1,0:T(8,128)(2,1)} %get-tuple-element.33), channel_id=1, source_target_pairs={{0,8},{8,16},{16,24},{24,32},{32,40},{40,48},{48,56},{56,64},{64,7... | collective-permute-start | bytes 9224 | tf_op jit(solution)/shard_map/ppermute | solution.py:61
  15.6 39.8 %collective-permute-start.1 = (bf16[3,2,1,512]{3,2,1,0:T(2,128)(2,1)}, bf16[3,2,1,512]{3,2,1,0:T(2,128)(2,1)S(1)}, u32[]{:S(2)}, u32[]{:S(2)}) collective-permute-start(bf16[3,2,1,512]{3,2,1,0:T(2,128)(2,1)} %get-tuple-element.32), channel_id=1, source_target_pairs={{1,0},{2,1},{3,2},{4,3},{5,4},{6,5},{7,6},{9,8},{10,9},{11,10},{12... | collective-permute-start | bytes 18440 | tf_op jit(solution)/shard_map/ppermute | solution.py:64
  17.7 38.3 %collective-permute-start = (bf16[3,2,1,512]{3,2,1,0:T(2,128)(2,1)}, bf16[3,2,1,512]{3,2,1,0:T(2,128)(2,1)}, u32[]{:S(2)}, u32[]{:S(2)}) collective-permute-start(bf16[3,2,1,512]{3,2,1,0:T(2,128)(2,1)} %get-tuple-element.31), channel_id=1, source_target_pairs={{0,1},{1,2},{2,3},{3,4},{4,5},{5,6},{6,7},{8,9},{9,10},{10,11},{11... | collective-permute-start | bytes 18440 | tf_op jit(solution)/shard_map/ppermute | solution.py:61
  26.7 35.6 %all-to-all-start = ((f32[32,256,4]{1,2,0:T(4,128)}), f32[32,256,4]{1,2,0:T(4,128)S(1)}, u32[]{:S(2)}, u32[]{:S(2)}) async-start(f32[32,256,4]{1,2,0:T(4,128)} %bitcast.63), calls=%async_computation | async-start | bytes 262144 | tf_op jit(solution)/shard_map/all_to_all | solution.py:22
  43.0 0.5 copy-start.14
  48.9 2.5 %copy-start.12 = (f32[256]{0:T(256)S(1)}, f32[256]{0:T(256)}, u32[]{:S(2)}) copy-start(f32[256]{0:T(256)} %get-tuple-element.7) | copy-start | bytes 3076
  48.9 2.5 %copy-start.18 = (f32[256]{0:T(256)S(1)}, f32[256]{0:T(256)}, u32[]{:S(2)}) copy-start(f32[256]{0:T(256)} %get-tuple-element.6) | copy-start | bytes 3076
  52.9 3.1 %copy-start.9 = (bf16[3,2,256,512]{3,2,1,0:T(8,128)(2,1)S(1)}, bf16[3,2,256,512]{3,2,1,0:T(8,128)(2,1)}, u32[]{:S(2)}) copy-start(bf16[3,2,256,512]{3,2,1,0:T(8,128)(2,1)} %copy-done.8) | copy-start | bytes 4718596
  52.9 4.2 %copy-start.2 = (f32[2,256,512]{2,1,0:T(8,128)S(1)}, f32[2,256,512]{2,1,0:T(8,128)}, u32[]{:S(2)}) copy-start(f32[2,256,512]{2,1,0:T(8,128)} %param.7) | copy-start | bytes 3145732
  52.9 4.2 %copy-start.4 = (f32[2,256,512]{2,1,0:T(8,128)S(1)}, f32[2,256,512]{2,1,0:T(8,128)}, u32[]{:S(2)}) copy-start(f32[2,256,512]{2,1,0:T(8,128)} %param.6) | copy-start | bytes 3145732
  55.4 0.6 copy-start.11
  57.0 0.9 copy-start.10
  57.1 0.9 copy-start.16
  57.1 0.9 copy-start.17
  64.2 12.2 %all-to-all-start.1 = ((bf16[8,256,4]{1,2,0:T(4,128)(2,1)}), bf16[8,256,4]{1,2,0:T(4,128)(2,1)S(1)}, u32[]{:S(2)}, u32[]{:S(2)}) async-start(bf16[8,256,4]{1,2,0:T(4,128)(2,1)} %broadcast_in_dim.2), calls=%async_computation.1 | async-start | bytes 32768 | tf_op jit(solution)/shard_map/all_to_all | solution.py:34
  76.4 130.0 %copy-start.21 = (f32[256]{0:T(256)S(1)}, f32[256]{0:T(256)}, u32[]{:S(2)}) copy-start(f32[256]{0:T(256)} %get-tuple-element.41) | copy-start | bytes 3076
  76.5 131.5 %copy-start.15 = (f32[256]{0:T(256)S(1)}, f32[256]{0:T(256)}, u32[]{:S(2)}) copy-start(f32[256]{0:T(256)} %copy-done.14) | copy-start | bytes 3076
  77.1 132.6 %copy-start.13 = (f32[256]{0:T(256)S(1)}, f32[256]{0:T(256)}, u32[]{:S(2)}) copy-start(f32[256]{0:T(256)} %get-tuple-element.7) | copy-start | bytes 3076
  203.9 5.9 %copy-start.3 = (f32[2,256,512]{2,1,0:T(8,128)S(1)}, f32[2,256,512]{2,1,0:T(8,128)}, u32[]{:S(2)}) copy-start(f32[2,256,512]{2,1,0:T(8,128)} %param.7) | copy-start | bytes 3145732
  203.9 5.9 %copy-start.5 = (f32[2,256,512]{2,1,0:T(8,128)S(1)}, f32[2,256,512]{2,1,0:T(8,128)}, u32[]{:S(2)}) copy-start(f32[2,256,512]{2,1,0:T(8,128)} %param.6) | copy-start | bytes 3145732
  207.9 2.6 %copy-start.7 = (f32[3,2,256,513]{3,2,1,0:T(8,128)S(1)}, f32[3,2,256,513]{3,2,1,0:T(8,128)}, u32[]{:S(2)}) copy-start(f32[3,2,256,513]{3,2,1,0:T(8,128)} %fusion.1) | copy-start | bytes 9455620
  209.8 2.0 copy-start.6
  209.8 2.0 copy-start.19
  209.8 2.0 copy-start.20
  209.8 2.0 copy-start.22
where the time goes:
time: 216 us; the launch traced here: 215 us
  blocking collectives  123 us (57%)
  other arithmetic  33.3 us (15%)
  starting transfers between devices  31.9 us (15%)
  local copies, waits for them, and re-layouts  15.9 us (7%)
  matrix products  10.4 us (5%)
    all_gather x1, blocking collectives, rows_first(): lax.all_gather(both, axis, axis=0, tiled=True)  123 us
    ppermute x2, starting transfers between devices, extended(): lax.ppermute(lax.slice_in_dim(block, 0, width, axis=dim), axis, backward)  13 us
    all_to_all x1, starting transfers between devices, sum_at_owner(): lax.all_to_all(blocks, axis, split_axis=0, concat_axis=0, tiled=True)  11.8 us
    mul x1, other arithmetic, tendency(): weighted = flux_rad * face_radius[:, None]  7.43 us
    all_to_all x1, starting transfers between devices, copy_for_each(): lax.all_to_all(jnp.broadcast_to(shard[None], (size, *shard.shape)), axis,...  4.81 us
  transfers between devices with their start and end apart: 6, of which 0 were waited for; matrix products, arithmetic and copies ran while one was open for 17% of the time, Pallas kernels for 0%

commit v1 on v0

v1 whole, which is shorter than its diff:
```python
import math

import jax
import jax.numpy as jnp
import ml_dtypes
import numpy as np
from jax import lax
from jax.experimental import pallas as pl
from jax.experimental.pallas import tpu as pltpu
from jax.sharding import PartitionSpec as P

NR = 2048
NAZ = 16384
MODES = 64
AZ = 32
RAD = 8
HALF = 16
LAYERS = 2
ROWS = NR // RAD
CELLS = NAZ // AZ
STEP = 2.0 * math.pi / NAZ
ASPECT_SQ = 0.0025
MESH = pl.DeviceIdType.MESH
F32 = jnp.float32
BF16 = jnp.bfloat16
NT = (((1,), (1,)), ((), ()))
NN = (((1,), (0,)), ((), ()))


def split(table):
    high = table.astype(ml_dtypes.bfloat16)
    low = (table - high.astype(np.float64)).astype(ml_dtypes.bfloat16)
    return (high, low)


def mode_tables():
    p, h, j = np.meshgrid(np.arange(16), np.arange(2), np.arange(4), indexing="ij")
    column = (4 * (16 * h + p) + j).reshape(-1)
    mode = (column // 2).astype(np.float64)
    odd = (column % 2).astype(bool)
    azimuth = (np.arange(NAZ) + 0.5) * STEP
    angle = mode[:, None] * azimuth[None, :]
    cos, sin = np.cos(angle), np.sin(angle)
    basis = np.where(odd[:, None], sin, cos)
    slope = np.where(odd[:, None], mode[:, None] * cos, -mode[:, None] * sin)
    tables = np.stack([*split(basis), *split(slope)])
    return np.ascontiguousarray(tables.reshape(4, 128, AZ, CELLS).transpose(2, 0, 1, 3))


def row_table():
    face = np.exp(np.arange(NR + 1) * STEP)
    inner, outer = face[:-1], face[1:]
    mid = 0.5 * (inner + outer)
    area = 0.5 * (outer * outer - inner * inner)
    table = np.zeros((NR, 128), np.float32)
    columns = [
        ASPECT_SQ / outer,
        np.sqrt(ASPECT_SQ / outer),
        0.05 * STEP * outer / area,
        0.05 * STEP * inner / area,
        ASPECT_SQ / mid,
        np.sqrt(ASPECT_SQ / mid),
        0.05 / mid,
        0.1 * STEP / mid,
        0.1 * STEP * (ASPECT_SQ / mid / mid - 1.0 / (mid * mid)),
        -0.1 / mid,
        ASPECT_SQ / inner,
        np.sqrt(ASPECT_SQ / inner),
    ]
    for k, values in enumerate(columns):
        table[:, k] = values
    return table


def face_flux(low, high, sound, sound_root, pressed):
    rho_l, mr_l, mp_l, v_l = low
    rho_h, mr_h, mp_h, v_h = high
    speed = jnp.maximum(jnp.abs(v_l), jnp.abs(v_h)) + sound_root
    a, b = v_l + speed, v_h - speed
    flux = [rho_l * a + rho_h * b, mr_l * a + mr_h * b, mp_l * a + mp_h * b]
    flux[pressed] = flux[pressed] + sound * (rho_l + rho_h)
    return flux


def exchange(
    density,
    mom_r,
    mom_phi,
    pot_kernel,
    force_kernel,
    tables,
    rows,
    coef,
    part,
    fluid,
    tab,
    kern,
    rtab,
    surf,
    chunks,
    arrived,
    halfsum,
    gathered,
    az_out,
    az_in,
    rad_out,
    rad_in,
    az_cols,
    carry,
    load_sem,
    send_sem,
    recv_sem,
    edge_send,
    edge_recv,
):
    az = lax.axis_index("az")
    rad = lax.axis_index("rad")
    z_hi = az // HALF
    p = az % HALF
    q = z_hi * RAD + rad
    az_next, az_prev = (az + 1) % AZ, (az + AZ - 1) % AZ
    rad_next, rad_prev = (rad + 1) % RAD, (rad + RAD - 1) % RAD
    plane = [(z_hi * HALF + (p + k) % HALF, rad) for k in range(1, HALF)]
    column = [
        (((q + k) % 16) // RAD * HALF + p, ((q + k) % 16) % RAD) for k in range(1, 16)
    ]
    partner = ((az + HALF) % AZ, rad)

    inside = pl.ds(8, ROWS)
    loads = [
        pltpu.make_async_copy(density, fluid.at[0, :, inside, :], load_sem.at[0]),
        pltpu.make_async_copy(tables.at[az], tab, load_sem.at[1]),
        pltpu.make_async_copy(mom_r, fluid.at[1, :, inside, :], load_sem.at[2]),
        pltpu.make_async_copy(mom_phi, fluid.at[2, :, inside, :], load_sem.at[3]),
        pltpu.make_async_copy(rows.at[pl.ds(rad * ROWS, ROWS), :], rtab, load_sem.at[4]),
        pltpu.make_async_copy(pot_kernel, kern.at[0], load_sem.at[5]),
        pltpu.make_async_copy(force_kernel, kern.at[1], load_sem.at[6]),
    ]
    for load in loads:
        load.start()

    barrier = pltpu.get_barrier_semaphore()
    greeted = plane + column + [(az_next, rad), (az_prev, rad)]
    for device in greeted:
        pl.semaphore_signal(barrier, inc=1, device_id=device, device_id_type=MESH)

    loads[0].wait()

    @pl.loop(0, ROWS // 32)
    def _(block):
        at = pl.multiple_of(block * 32, 32)
        value = fluid[0, 0, pl.ds(8 + at, 32), :] + fluid[0, 1, pl.ds(8 + at, 32), :]
        high = value.astype(BF16)
        surf[0, pl.ds(at, 32), :] = high
        surf[1, pl.ds(at, 32), :] = (value - high.astype(F32)).astype(BF16)

    loads[1].wait()
    share = lax.dot_general(tab[0], surf[0], NT, preferred_element_type=F32)
    share += lax.dot_general(tab[0], surf[1], NT, preferred_element_type=F32)
    share += lax.dot_general(tab[1], surf[0], NT, preferred_element_type=F32)
    chunks[...] = share.reshape(HALF, 8, ROWS)

    pl.semaphore_wait(barrier, len(greeted))

    sends = []
    for k, (az_to, rad_to) in enumerate(plane):
        copy = pltpu.make_async_remote_copy(
            src_ref=chunks.at[(p + k + 1) % HALF],
            dst_ref=arrived.at[k],
            send_sem=send_sem.at[0],
            recv_sem=recv_sem.at[0],
            device_id=(az_to, rad_to),
            device_id_type=MESH,
        )
        copy.start()

    loads[2].wait()
    loads[3].wait()
    row_id = lax.broadcasted_iota(jnp.int32, (8, 128), 0)
    lane_id = lax.broadcasted_iota(jnp.int32, (8, 128), 1)
    for side, (lanes, lane) in enumerate(((pl.ds(0, 128), 0), (pl.ds(CELLS - 128, 128), 127))):
        total = jnp.zeros((8, ROWS), F32)
        for f in range(6):
            pick = jnp.where((row_id == f) & (lane_id == lane), 1.0, 0.0).astype(BF16)
            block = fluid[f // 2, f % 2, inside, lanes].astype(BF16)
            total += lax.dot_general(pick, block, NT, preferred_element_type=F32)
        az_out[side] = total
    for f in range(6):
        rad_out[0, f : f + 1, :] = fluid[f // 2, f % 2, 8:9, :]
        rad_out[1, f : f + 1, :] = fluid[f // 2, f % 2, 8 + ROWS - 1 : 8 + ROWS, :]
    rad_out[0, 6:8, :] = jnp.zeros((2, CELLS), F32)
    rad_out[1, 6:8, :] = jnp.zeros((2, CELLS), F32)
    edges = []
    for n, (src, dst, device) in enumerate(
        (
            (az_out.at[0], az_in.at[1], (az_prev, rad)),
            (az_out.at[1], az_in.at[0], (az_next, rad)),
            (rad_out.at[0], rad_in.at[1], (az, rad_prev)),
            (rad_out.at[1], rad_in.at[0], (az, rad_next)),
        )
    ):
        copy = pltpu.make_async_remote_copy(
            src_ref=src,
            dst_ref=dst,
            send_sem=edge_send.at[n],
            recv_sem=edge_recv.at[n],
            device_id=device,
            device_id_type=MESH,
        )
        copy.start()
        edges.append(copy)

    fifteen = arrived.at[pl.ds(0, 15)]
    pltpu.make_async_copy(fifteen, fifteen, recv_sem.at[0]).wait()
    total = chunks[p]
    for k in range(15):
        total = total + arrived[k]
    for h in range(2):
        halfsum[h, 0:4, :] = total[4 * h : 4 * h + 4, 0:128]
        halfsum[h, 4:8, :] = total[4 * h : 4 * h + 4, 128:256]
    gathered[q] = halfsum[z_hi]
    for k, (az_to, rad_to) in enumerate(column):
        copy = pltpu.make_async_remote_copy(
            src_ref=halfsum.at[az_to // HALF],
            dst_ref=gathered.at[q],
            send_sem=send_sem.at[1],
            recv_sem=recv_sem.at[1],
            device_id=(az_to, rad_to),
            device_id_type=MESH,
        )
        copy.start()

    loads[4].wait()
    for edge in edges:
        edge.wait()
    az_cols[0] = az_in[0].T
    az_cols[1] = az_in[1].T
    for f in range(6):
        field, layer = f // 2, f % 2
        inner = jnp.where(rad == 0, rad_out[0, f : f + 1, :], rad_in[0, f : f + 1, :])
        outer = jnp.where(rad == RAD - 1, rad_out[1, f : f + 1, :], rad_in[1, f : f + 1, :])
        fluid[field, layer, 0:8, :] = jnp.broadcast_to(inner, (8, CELLS))
        fluid[field, layer, 8 + ROWS : 16 + ROWS, :] = jnp.broadcast_to(outer, (8, CELLS))

    wide_row = lax.broadcasted_iota(jnp.int32, (8, CELLS), 0)
    wide_lane = lax.broadcasted_iota(jnp.int32, (8, CELLS), 1)

    def state(layer, at):
        rho = fluid[0, layer, pl.ds(at, 8), :]
        mr = fluid[1, layer, pl.ds(at, 8), :]
        mp = fluid[2, layer, pl.ds(at, 8), :]
        return (rho, mr, mp)

    def up(now, later):
        return pltpu.roll(jnp.where(wide_row == 0, later, now), 7, 0)

    def radial(now, later, sound, sound_root):
        inv_now, inv_later = 1.0 / now[0], 1.0 / later[0]
        low = (*now, now[1] * inv_now)
        late = (*later, later[1] * inv_later)
        high = [up(a, b) for a, b in zip(low, late)]
        return face_flux(low, high, sound, sound_root, 1), inv_now

    for layer in range(LAYERS):
        flux, _ = radial(
            state(layer, 0), state(layer, 8), rtab[0:1, 10:11], rtab[0:1, 11:12]
        )
        for c in range(3):
            carry[c, layer] = flux[c]

    def update(block):
        at = pl.multiple_of(block * 8, 8)
        here = pl.ds(at, 8)

        def factor(k):
            return jnp.broadcast_to(rtab[here, k : k + 1], (8, CELLS))

        for layer in range(LAYERS):
            now, later = state(layer, at + 8), state(layer, at + 16)
            flux, inv = radial(now, later, factor(0), factor(1))
            rho, mr, mp = now
            vp = mp * inv
            cells = (rho, mr, mp, vp)
            left = []
            for c in range(4):
                left.append(pltpu.roll(cells[c], 1, 1))
            lo_cols = [az_cols[0, here, 2 * c + layer : 2 * c + layer + 1] for c in range(3)]
            hi_cols = [az_cols[1, here, 2 * c + layer : 2 * c + layer + 1] for c in range(3)]
            lo_cols.append(lo_cols[2] / lo_cols[0])
            hi_cols.append(hi_cols[2] / hi_cols[0])
            left = [jnp.where(wide_lane == 0, jnp.broadcast_to(a, (8, CELLS)), b) for a, b in zip(lo_cols, left)]
            aflux = face_flux(left, cells, factor(4), factor(5), 2)
            last = [cell[:, CELLS - 1 :] for cell in cells]
            lflux = face_flux(last, hi_cols, rtab[here, 4:5], rtab[here, 5:6], 2)
            new = []
            for c in range(3):
                below = pltpu.roll(jnp.where(wide_row == 7, carry[c, layer], flux[c]), 1, 0)
                above = pltpu.roll(aflux[c], CELLS - 1, 1)
                above = jnp.where(wide_lane == CELLS - 1, jnp.broadcast_to(lflux[c], (8, CELLS)), above)
                change = factor(2) * flux[c] - factor(3) * below + factor(6) * (above - aflux[c])
                carry[c, layer] = flux[c]
                new.append(now[c] - change)
            turn = factor(7) * vp
            new[1] = new[1] + (turn * mp + factor(8) * rho)
            new[2] = new[2] - turn * mr
            for c in range(3):
                part[c, layer, here, :] = new[c]

    def update_range(start, stop):
        @pl.loop(start, stop)
        def _(block):
            update(block)

    update_range(0, 12)

    loads[5].wait()
    loads[6].wait()
    fifteen = gathered.at[pl.ds(0, 15)]
    pltpu.make_async_copy(fifteen, fifteen, recv_sem.at[1]).wait()
    pieces = []
    for r in range(RAD):
        both = (gathered[r] + gathered[RAD + r]) * (1.0 / NAZ)
        pieces += [both[0:4], both[4:8]]
    modes = jnp.concatenate(pieces, axis=1)
    modes = jnp.concatenate([modes, jnp.zeros_like(modes)], axis=0).astype(BF16)
    for which in range(2):
        for m in range(2):
            product = lax.dot_general(modes, kern[which, m], NT, preferred_element_type=F32)
            coef[az, 4 * which + 2 * m : 4 * which + 2 * m + 2, :] = product[2 * m : 2 * m + 2, :]

    cross = pltpu.make_async_remote_copy(
        src_ref=coef.at[az],
        dst_ref=coef.at[az],
        send_sem=send_sem.at[2],
        recv_sem=recv_sem.at[2],
        device_id=partner,
        device_id_type=MESH,
    )
    cross.start()
    for az_to, rad_to in plane:
        pltpu.make_async_remote_copy(
            src_ref=coef.at[az],
            dst_ref=coef.at[az],
            send_sem=send_sem.at[3],
            recv_sem=recv_sem.at[3],
            device_id=(az_to, rad_to),
            device_id_type=MESH,
        ).start()
    update_range(12, 20)
    cross.wait_recv()
    for az_to, rad_to in plane:
        pltpu.make_async_remote_copy(
            src_ref=coef.at[partner[0]],
            dst_ref=coef.at[partner[0]],
            send_sem=send_sem.at[4],
            recv_sem=recv_sem.at[4],
            device_id=(az_to, rad_to),
            device_id_type=MESH,
        ).start()
    update_range(20, 32)

    fifteen = coef.at[pl.ds(0, 15)]
    pltpu.make_async_copy(fifteen, fifteen, recv_sem.at[3]).wait()
    pltpu.make_async_copy(fifteen, fifteen, recv_sem.at[4]).wait()
    cross.wait_send()
    for n in (0, 3, 4):
        pltpu.make_async_copy(fifteen, fifteen, send_sem.at[n]).wait()
    fifteen = gathered.at[pl.ds(0, 15)]
    pltpu.make_async_copy(fifteen, fifteen, send_sem.at[1]).wait()


def finish(coef, part, fluid, tab, rtab, out_density, out_r, out_phi, out_pot, pot_buf, mom_buf, sem):
    first = pltpu.make_async_copy(part.at[0], out_density, sem.at[0])
    first.start()
    row_id = lax.broadcasted_iota(jnp.int32, (8, ROWS), 0)
    pots, forces = [], []
    for n in range(HALF):
        a, b = coef[n], coef[HALF + n]
        pots.append(jnp.where(row_id < 4, a, pltpu.roll(b, 4, 0)))
        forces.append(jnp.where(row_id < 4, pltpu.roll(a, 4, 0), b))

    def sides(tiles):
        value = jnp.concatenate(tiles, axis=0).T
        high = value.astype(BF16)
        return high, (value - high.astype(F32)).astype(BF16)

    def product(sides, table, rows):
        high, low = sides[0][rows], sides[1][rows]
        out = lax.dot_general(high, tab[table], NN, preferred_element_type=F32)
        out += lax.dot_general(low, tab[table], NN, preferred_element_type=F32)
        return out + lax.dot_general(high, tab[table + 1], NN, preferred_element_type=F32)

    pot, force = sides(pots), sides(forces)
    block = 64
    copies = []
    for n in range(ROWS // block):
        here = slice(n * block, (n + 1) * block)
        pot_buf[here, :] = product(pot, 0, here)
        radial = 0.1 * product(force, 0, here)
        azimuthal = product(pot, 2, here) * rtab[here, 9:10]
        inside = slice(8 + n * block, 8 + (n + 1) * block)
        for layer in range(LAYERS):
            rho = fluid[0, layer, inside, :]
            mom_buf[0, layer, here, :] = part[1, layer, here, :] + rho * radial
            mom_buf[1, layer, here, :] = part[2, layer, here, :] + rho * azimuthal
        for k, (src, dst) in enumerate(
            (
                (pot_buf.at[pl.ds(n * block, block), :], out_pot.at[pl.ds(n * block, block), :]),
                (mom_buf.at[0, :, pl.ds(n * block, block), :], out_r.at[:, pl.ds(n * block, block), :]),
                (mom_buf.at[1, :, pl.ds(n * block, block), :], out_phi.at[:, pl.ds(n * block, block), :]),
            )
        ):
            copy = pltpu.make_async_copy(src, dst, sem.at[1 + 3 * n + k])
            copy.start()
            copies.append(copy)
    first.wait()
    for copy in copies:
        copy.wait()


def local(density, mom_r, mom_phi, potential_kernel, force_kernel):
    tables = jnp.asarray(mode_tables())
    rows = jnp.asarray(row_table())
    operands = (density, mom_r, mom_phi, potential_kernel, force_kernel, tables, rows)
    hbm = pl.BlockSpec(memory_space=pltpu.HBM)
    vmem = pl.BlockSpec(memory_space=pltpu.VMEM)
    dma = pltpu.SemaphoreType.DMA
    shared = (
        ((AZ, 8, ROWS), F32),
        ((3, LAYERS, ROWS, CELLS), F32),
        ((3, LAYERS, ROWS + 16, CELLS), F32),
        ((4, 128, CELLS), BF16),
        ((ROWS, 128), F32),
    )
    coef, part, fluid, tab, rtab = pl.pallas_call(
        exchange_call,
        out_shape=[pltpu.VMEM(shape, dtype) for shape, dtype in shared],
        in_specs=[hbm] * 7,
        out_specs=[vmem] * 5,
        scratch_shapes=[
            pltpu.VMEM((2, 2, ROWS, NR), BF16),
            pltpu.VMEM((2, ROWS, CELLS), BF16),
            pltpu.VMEM((HALF, 8, ROWS), F32),
            pltpu.VMEM((15, 8, ROWS), F32),
            pltpu.VMEM((2, 8, 128), F32),
            pltpu.VMEM((16, 8, 128), F32),
            pltpu.VMEM((2, 8, ROWS), F32),
            pltpu.VMEM((2, 8, ROWS), F32),
            pltpu.VMEM((2, 8, CELLS), F32),
            pltpu.VMEM((2, 8, CELLS), F32),
            pltpu.VMEM((2, ROWS, 8), F32),
            pltpu.VMEM((3, LAYERS, 8, CELLS), F32),
            dma((7,)),
            dma((5,)),
            dma((5,)),
            dma((4,)),
            dma((4,)),
        ],
        compiler_params=pltpu.CompilerParams(
            collective_id=0, has_side_effects=True, vmem_limit_bytes=32 * 2**20
        ),
        name="exchange",
    )(*(pltpu.with_memory_space_constraint(a, pltpu.HBM) for a in operands))
    fluid_shape = jax.ShapeDtypeStruct((LAYERS, ROWS, CELLS), F32)
    return pl.pallas_call(
        finish,
        out_shape=[fluid_shape, fluid_shape, fluid_shape, jax.ShapeDtypeStruct((ROWS, CELLS), F32)],
        in_specs=[vmem] * 5,
        out_specs=[hbm] * 4,
        scratch_shapes=[
            pltpu.VMEM((ROWS, CELLS), F32),
            pltpu.VMEM((2, LAYERS, ROWS, CELLS), F32),
            dma((1 + 3 * 4,)),
        ],
        compiler_params=pltpu.CompilerParams(vmem_limit_bytes=32 * 2**20),
        name="finish",
    )(coef, part, fluid, tab, rtab)


def exchange_call(d, r, f, pk, fk, tables, rows, coef, part, fluid, tab, rtab, kern, *rest):
    exchange(d, r, f, pk, fk, tables, rows, coef, part, fluid, tab, kern, rtab, *rest)


def solution(mesh):
    fluid = P(None, "rad", "az")
    kernel = P("az", "rad", None)
    return jax.shard_map(
        local,
        mesh=mesh,
        in_specs=(fluid, fluid, fluid, kernel, kernel),
        out_specs=(fluid, fluid, fluid, P("rad", "az")),
        check_vma=False,
    )
```

time: 216 us -> 38.2 us (0.18)
  blocking collectives: 123 us -> 0 us
  Pallas kernels: 0 us -> 37.4 us
  other arithmetic: 33.3 us -> 0 us
  starting transfers between devices: 31.9 us -> 0 us
  local copies, waits for them, and re-layouts: 15.9 us -> 0 us
  matrix products: 10.4 us -> 0 us
    all_gather x1 -> x0, blocking collectives: 123 us -> none  [rows_first(): lax.all_gather(both, axis, axis=0, tiled=True)]
    pallas_call x0 -> x2, Pallas kernels: none -> 37.4 us  [the longest x1 35.4 us: local(): pl.pallas_call(exchange_call, out_shape=[pltpu.VMEM(shape, dtype) for sha...]
    all_to_all x2 -> x0, starting transfers between devices: 16.6 us -> none  [the longest x1 11.8 us: sum_at_owner(): lax.all_to_all(blocks, axis, split_axis=0, concat_axis=0, tiled=True)]
    ppermute x4 -> x0, starting transfers between devices: 15.3 us -> none  [the longest x2 13 us: extended(): lax.ppermute(lax.slice_in_dim(block, 0, width, axis=dim), axis, backward)]
    mul x4 -> x0, other arithmetic: 12.4 us -> none  [the longest x1 7.43 us: tendency(): weighted = flux_rad * face_radius[:, None]]
    dot_general x6 -> x0, matrix products: 10.4 us -> none  [the longest x1 2.46 us: local(): potential = jnp.dot(portion[0], basis_rows, precision=highest)]
    another operation x3 -> x0, other arithmetic: 5.26 us -> none  [the longest x1 3.81 us: local(): fields = jnp.stack([density, mom_r, mom_phi])]
    convert_element_type x3 -> x0, other arithmetic: 4.81 us -> none  [the longest x1 2.46 us: local(): extended(fields.astype(jnp.bfloat16), (('az', 3),), 1, True)]
  transfers between devices with their start and end apart: 6 -> 0, of which waited for: 0 -> 0; matrix products, arithmetic and copies ran while one was open for 17% -> 0% of each run, Pallas kernels for 0% -> 0%
where the time goes in v1:
time: 38.2 us; the launch traced here: 38 us
  Pallas kernels  37.4 us (98%)
  between operations  0.64 us (2%)
    pallas_call x1, Pallas kernels, local(): pl.pallas_call(exchange_call, out_shape=[pltpu.VMEM(shape, dtype) for sha...  35.4 us
    pallas_call x1, Pallas kernels, local(): pl.pallas_call(finish, out_shape=[fluid_shape, fluid_shape, fluid_shape,...  1.95 us

profile of v1, /device:TPU:32, one launch (start us, length us, event | category | flops | bytes accessed | tf_op | source)
XLA Modules:
  0.0 38.0 jit_solution(10724773863113694852)
XLA Ops:
  0.6 35.4 %exchange.1 = (f32[32,8,256]{2,1,0:T(8,128)S(1)}, f32[3,2,256,512]{3,2,1,0:T(8,128)S(1)}, f32[3,2,272,512]{3,2,1,0:T(8,128)S(1)}, bf16[4,128,512]{2,1,0:T(8,128)(2,1)S(1)}, f32[256,128]{1,0:T(8,128)S(1)}) custom-call(f32[2,256,512]{2,1,0:T(8,128)} %d.1, f32[2,256,512]{2,1,0:T(8,128)} %r.1, f32[2,256,512]{2,1,0:T(8,128)} %f.1, bf16[2,256,2048]{2,1,0:T(8,128)(2,1)} %pk.1, ...), custom_call_target="tpu_custom_call" | custom-call | tf_op jit(solution)/shard_map/exchange/pallas_call | solution.py:435
  36.0 2.0 %finish.1 = (f32[2,256,512]{2,1,0:T(8,128)}, f32[2,256,512]{2,1,0:T(8,128)}, f32[2,256,512]{2,1,0:T(8,128)}, f32[256,512]{1,0:T(8,128)}) custom-call(f32[32,8,256]{2,1,0:T(8,128)S(1)} %get-tuple-element.9.coef, f32[3,2,256,512]{3,2,1,0:T(8,128)S(1)} %get-tuple-element.10.part, f32[3,2,272,512]{3,2,1,0:T(8,128)S(1)} %get-tuple-element.11.fluid, ...), custom_call_target="tpu_custom_call" | custom-call | tf_op jit(solution)/shard_map/finish/pallas_call | solution.py:465

commit v2 on v1

v2 whole, which is shorter than its diff:
```python
import math

import jax
import jax.numpy as jnp
import ml_dtypes
import numpy as np
from jax import lax
from jax.experimental import pallas as pl
from jax.experimental.pallas import tpu as pltpu
from jax.sharding import PartitionSpec as P

NR = 2048
NAZ = 16384
MODES = 64
AZ = 32
RAD = 8
HALF = 16
LAYERS = 2
ROWS = NR // RAD
CELLS = NAZ // AZ
STEP = 2.0 * math.pi / NAZ
ASPECT_SQ = 0.0025
MESH = pl.DeviceIdType.MESH
F32 = jnp.float32
BF16 = jnp.bfloat16
NT = (((1,), (1,)), ((), ()))
NN = (((1,), (0,)), ((), ()))


def split(table):
    high = table.astype(ml_dtypes.bfloat16)
    low = (table - high.astype(np.float64)).astype(ml_dtypes.bfloat16)
    return (high, low)


def mode_tables():
    p, h, j = np.meshgrid(np.arange(16), np.arange(2), np.arange(4), indexing="ij")
    column = (4 * (16 * h + p) + j).reshape(-1)
    mode = (column // 2).astype(np.float64)
    odd = (column % 2).astype(bool)
    azimuth = (np.arange(NAZ) + 0.5) * STEP
    angle = mode[:, None] * azimuth[None, :]
    cos, sin = np.cos(angle), np.sin(angle)
    basis = np.where(odd[:, None], sin, cos)
    slope = np.where(odd[:, None], mode[:, None] * cos, -mode[:, None] * sin)
    tables = np.stack([*split(basis), *split(slope)])
    return np.ascontiguousarray(tables.reshape(4, 128, AZ, CELLS).transpose(2, 0, 1, 3))


def row_tables():
    face = np.exp(np.arange(NR + 1) * STEP)
    inner, outer = face[:-1], face[1:]
    mid = 0.5 * (inner + outer)
    area = 0.5 * (outer * outer - inner * inner)
    table = np.zeros((NR, 128), np.float32)
    columns = [
        ASPECT_SQ / outer,
        np.sqrt(ASPECT_SQ / outer),
        0.05 * STEP * outer / area,
        0.05 * STEP * inner / area,
        ASPECT_SQ / mid,
        np.sqrt(ASPECT_SQ / mid),
        0.05 / mid,
        0.1 * STEP / mid,
        0.1 * STEP * (ASPECT_SQ / mid / mid - 1.0 / (mid * mid)),
        -0.1 / mid,
        ASPECT_SQ / inner,
        np.sqrt(ASPECT_SQ / inner),
    ]
    for k, values in enumerate(columns):
        table[:, k] = values
    across = np.zeros((8, NR), np.float32)
    for k, n in enumerate((4, 5, 6)):
        across[k] = columns[n]
    return (table, across)


def face_flux(low, high, sound, sound_root, pressed):
    rho_l, mr_l, mp_l, v_l = low
    rho_h, mr_h, mp_h, v_h = high
    speed = jnp.maximum(jnp.abs(v_l), jnp.abs(v_h)) + sound_root
    a, b = v_l + speed, v_h - speed
    flux = [rho_l * a + rho_h * b, mr_l * a + mr_h * b, mp_l * a + mp_h * b]
    flux[pressed] = flux[pressed] + sound * (rho_l + rho_h)
    return flux


def reciprocal(value):
    guess = pl.reciprocal(value, approx=True)
    return guess * (2.0 - value * guess)


def whole(ref, count):
    slots = ref.at[pl.ds(0, count)]
    return lambda sem: pltpu.make_async_copy(slots, slots, sem).wait()


def radial_flux(low, high, sound, sound_root):
    return face_flux(
        (*low, low[1] * reciprocal(low[0])),
        (*high, high[1] * reciprocal(high[0])),
        sound,
        sound_root,
        1,
    )


def azimuth_flux(low, high, sound, sound_root):
    return face_flux(
        (*low, low[2] * reciprocal(low[0])),
        (*high, high[2] * reciprocal(high[0])),
        sound,
        sound_root,
        2,
    )


def pairs_of(ref, at):
    value = ref[at]
    return [value[2 * c : 2 * c + 2] for c in range(3)]


def exchange(
    density,
    mom_r,
    mom_phi,
    pot_kernel,
    force_kernel,
    tables,
    rows,
    lanes,
    coef,
    part,
    fluid,
    tab,
    rtab,
    kern,
    ltab,
    surf,
    chunks,
    arrived,
    halfsum,
    gathered,
    az_out,
    az_in,
    az_swap,
    rad_out,
    rad_in,
    carry,
    load_sem,
    send_sem,
    recv_sem,
    column_sem,
    edge_send,
    edge_recv,
):
    az = lax.axis_index("az")
    rad = lax.axis_index("rad")
    z_hi = az // HALF
    p = az % HALF
    y, x = p // 4, p % 4
    z, core = z_hi * 4 + rad // 2, rad % 2
    q = z_hi * RAD + rad
    partner = ((az + HALF) % AZ, rad)

    far = [(2, 2), (1, 2), (2, 1), (3, 2), (2, 3), (1, 1), (3, 3), (1, 3), (3, 1), (2, 0), (0, 2), (0, 1), (1, 0), (0, 3), (3, 0)]
    plane = [(y + dy) % 4 * 4 + (x + dx) % 4 for dy, dx in far]
    column = []
    for dz, dc in [(4, 0), (4, 1), (3, 0), (5, 0), (3, 1), (5, 1), (2, 0), (6, 0), (2, 1), (6, 1), (1, 0), (7, 0), (1, 1), (7, 1), (0, 1)]:
        there = (z + dz) % 8
        column.append((there // 4, there % 4 * 2 + (core + dc) % 2))

    barrier = pltpu.get_barrier_semaphore()
    for to in plane:
        pl.semaphore_signal(barrier, inc=1, device_id=(z_hi * HALF + to, rad), device_id_type=MESH)
    for half, to in column:
        pl.semaphore_signal(barrier, inc=1, device_id=(half * HALF + p, to), device_id_type=MESH)

    inside = pl.ds(8, ROWS)
    loads = [
        pltpu.make_async_copy(density, fluid.at[0, :, inside, :], load_sem.at[0]),
        pltpu.make_async_copy(tables.at[az], tab, load_sem.at[1]),
        pltpu.make_async_copy(mom_r, fluid.at[1, :, inside, :], load_sem.at[2]),
        pltpu.make_async_copy(mom_phi, fluid.at[2, :, inside, :], load_sem.at[3]),
        pltpu.make_async_copy(rows.at[pl.ds(rad * ROWS, ROWS), :], rtab, load_sem.at[4]),
        pltpu.make_async_copy(lanes.at[:, pl.ds(rad * ROWS, ROWS)], ltab, load_sem.at[5]),
        pltpu.make_async_copy(pot_kernel, kern.at[0], load_sem.at[6]),
        pltpu.make_async_copy(force_kernel, kern.at[1], load_sem.at[7]),
    ]
    for load in loads:
        load.start()

    loads[0].wait()

    @pl.loop(0, ROWS // 32)
    def _(block):
        at = pl.multiple_of(block * 32, 32)
        value = fluid[0, 0, pl.ds(8 + at, 32), :] + fluid[0, 1, pl.ds(8 + at, 32), :]
        high = value.astype(BF16)
        surf[0, pl.ds(at, 32), :] = high
        surf[1, pl.ds(at, 32), :] = (value - high.astype(F32)).astype(BF16)

    loads[1].wait()
    share = lax.dot_general(tab[0], surf[0], NT, preferred_element_type=F32)
    share += lax.dot_general(tab[0], surf[1], NT, preferred_element_type=F32)
    share += lax.dot_general(tab[1], surf[0], NT, preferred_element_type=F32)
    chunks[...] = share.reshape(HALF, 8, ROWS)

    pl.semaphore_wait(barrier, len(plane) + len(column))

    for k, to in enumerate(plane):
        pltpu.make_async_remote_copy(
            src_ref=chunks.at[to],
            dst_ref=arrived.at[k],
            send_sem=send_sem.at[0],
            recv_sem=recv_sem.at[0],
            device_id=(z_hi * HALF + to, rad),
            device_id_type=MESH,
        ).start()

    loads[2].wait()
    loads[3].wait()
    row_id = lax.broadcasted_iota(jnp.int32, (8, 256), 0)
    lane_id = lax.broadcasted_iota(jnp.int32, (8, 256), 1)
    for side, (at, lane) in enumerate(((0, 0), (CELLS - 128, 127))):
        total = jnp.zeros((8, ROWS), F32)
        for c in range(3):
            both = jnp.concatenate([fluid[c, n, inside, at : at + 128] for n in range(2)], axis=1)
            pick = jnp.where(lane_id == lane + 128 * (row_id - 2 * c), 1.0, 0.0)
            pick = jnp.where((row_id == 2 * c) | (row_id == 2 * c + 1), pick, 0.0).astype(BF16)
            high = both.astype(BF16)
            low = (both - high.astype(F32)).astype(BF16)
            total += lax.dot_general(pick, high, NT, preferred_element_type=F32)
            total += lax.dot_general(pick, low, NT, preferred_element_type=F32)
        az_out[side] = total
    rad_out[...] = jnp.zeros_like(rad_out)
    for f in range(6):
        rad_out[0, f : f + 1, :] = fluid[f // 2, f % 2, 8:9, :]
        rad_out[1, f : f + 1, :] = fluid[f // 2, f % 2, 8 + ROWS - 1 : 8 + ROWS, :]
    edges = []
    for n, (src, dst, device) in enumerate(
        (
            (az_out.at[0], az_in.at[1], (z_hi * HALF + (p + HALF - 1) % HALF, rad)),
            (az_out.at[1], az_in.at[0], (z_hi * HALF + (p + 1) % HALF, rad)),
            (rad_out.at[0], rad_in.at[1], (az, (rad + RAD - 1) % RAD)),
            (rad_out.at[1], rad_in.at[0], (az, (rad + 1) % RAD)),
        )
    ):
        copy = pltpu.make_async_remote_copy(
            src_ref=src,
            dst_ref=dst,
            send_sem=edge_send.at[n],
            recv_sem=edge_recv.at[n],
            device_id=device,
            device_id_type=MESH,
        )
        copy.start()
        edges.append(copy)

    loads[4].wait()
    for c in range(3):
        for layer in range(LAYERS):
            fluid[c, layer, 0:8, :] = jnp.broadcast_to(fluid[c, layer, 8:9, :], (8, CELLS))
            fluid[c, layer, 8 + ROWS : 16 + ROWS, :] = jnp.broadcast_to(
                fluid[c, layer, 7 + ROWS : 8 + ROWS, :], (8, CELLS)
            )
    for layer in range(LAYERS):
        edge = [fluid[c, layer, 0:8, :] for c in range(3)]
        flux = radial_flux(edge, edge, rtab[0:1, 10:11], rtab[0:1, 11:12])
        for c in range(3):
            carry[c, layer] = flux[c]

    size = 32

    @pl.loop(0, ROWS // size)
    def _(block):
        at = pl.multiple_of(block * size, size)
        here = pl.ds(at, size)

        def factor(k):
            return jnp.broadcast_to(rtab[here, k : k + 1], (size, CELLS))

        for layer in range(LAYERS):
            state = [fluid[c, layer, pl.ds(at + 8, size + 8), :] for c in range(3)]
            inv = reciprocal(state[0])
            state.append(state[1] * inv)
            low = [value[:size] for value in state]
            high = [pltpu.roll(value, size + 7, 0)[:size] for value in state]
            flux = face_flux(low, high, factor(0), factor(1), 1)
            rho, mr, mp = low[:3]
            vp = mp * inv[:size]
            cells = (rho, mr, mp, vp)
            left = [pltpu.roll(value, 1, 1) for value in cells]
            side = face_flux(left, cells, factor(4), factor(5), 2)
            new = []
            for c in range(3):
                below = pltpu.roll(jnp.concatenate([carry[c, layer], flux[c]], axis=0), 1, 0)[8:]
                above = pltpu.roll(side[c], CELLS - 1, 1)
                carry[c, layer] = flux[c][size - 8 :]
                new.append(
                    low[c]
                    - (factor(2) * flux[c] - factor(3) * below + factor(6) * (above - side[c]))
                )
            turn = factor(7) * vp
            new[1] = new[1] + (turn * mp + factor(8) * rho)
            new[2] = new[2] - turn * mr
            for c in range(3):
                part[c, layer, here, :] = new[c]

    whole(arrived, 15)(recv_sem.at[0])
    total = chunks[p]
    for k in range(15):
        total = total + arrived[k]
    for h in range(2):
        halfsum[h, 0:4, :] = total[4 * h : 4 * h + 4, 0:128]
        halfsum[h, 4:8, :] = total[4 * h : 4 * h + 4, 128:256]
    gathered[z_hi, rad] = halfsum[z_hi]
    for half, to in column:
        pltpu.make_async_remote_copy(
            src_ref=halfsum.at[half],
            dst_ref=gathered.at[z_hi, rad],
            send_sem=send_sem.at[1],
            recv_sem=column_sem.at[(rad - to + RAD) % RAD],
            device_id=(half * HALF + p, to),
            device_id_type=MESH,
        ).start()

    edges[2].wait()
    edges[3].wait()
    for side, (outermost, sign, weight, sound) in enumerate(
        ((rad == 0, 1.0, rtab[0:1, 3:4], 10), (rad == RAD - 1, -1.0, rtab[ROWS - 1 : ROWS, 2:3], 0))
    ):
        row = 0 if side == 0 else ROWS - 1
        sounds = (rtab[row : row + 1, sound : sound + 1], rtab[row : row + 1, sound + 1 : sound + 2])
        own = pairs_of(rad_out, side)
        beyond = [jnp.where(outermost, a, b) for a, b in zip(own, pairs_of(rad_in, side))]
        used = radial_flux(own, own, *sounds)
        right = radial_flux(beyond, own, *sounds) if side == 0 else radial_flux(own, beyond, *sounds)
        for c in range(3):
            delta = (sign * weight) * (right[c] - used[c])
            for layer in range(LAYERS):
                part[c, layer, row : row + 1, :] = part[c, layer, row : row + 1, :] + delta[layer : layer + 1]

    edges[0].wait()
    edges[1].wait()
    end = p // (HALF - 1)
    swap = pltpu.make_async_remote_copy(
        src_ref=az_in.at[end],
        dst_ref=az_swap,
        send_sem=edge_send.at[4],
        recv_sem=edge_recv.at[4],
        device_id=partner,
        device_id_type=MESH,
    )
    at_end = (p == 0) | (p == HALF - 1)

    @pl.when(at_end)
    def _():
        swap.start()

    loads[6].wait()
    loads[7].wait()
    products = [jnp.zeros((16, ROWS), F32) for _ in range(4)]
    for k in (0, 1, 7, 2, 6, 3, 5, 4):
        from_rad = (rad + k) % RAD
        pair = gathered.at[:, from_rad] if k else gathered.at[pl.ds(0, 1), from_rad]
        pltpu.make_async_copy(pair, pair, column_sem.at[k]).wait()
        both = (gathered[0, from_rad] + gathered[1, from_rad]) * (1.0 / NAZ)
        modes = jnp.concatenate([both[0:4], both[4:8]], axis=1)
        modes = jnp.concatenate([modes] * 4, axis=0).astype(BF16)
        at = pl.ds(pl.multiple_of(from_rad * ROWS, ROWS), ROWS)
        for n in range(4):
            products[n] += lax.dot_general(modes, kern[n // 2, n % 2, :, at], NT, preferred_element_type=F32)
    for n in range(4):
        m = n % 2
        coef[az, 2 * n : 2 * n + 2, :] = products[n][2 * m : 2 * m + 2]

    cross = pltpu.make_async_remote_copy(
        src_ref=coef.at[az],
        dst_ref=coef.at[az],
        send_sem=send_sem.at[2],
        recv_sem=recv_sem.at[1],
        device_id=partner,
        device_id_type=MESH,
    )
    cross.start()

    def to_plane(slot, n):
        for to in plane:
            pltpu.make_async_remote_copy(
                src_ref=coef.at[slot],
                dst_ref=coef.at[slot],
                send_sem=send_sem.at[1 + n],
                recv_sem=recv_sem.at[n],
                device_id=(z_hi * HALF + to, rad),
                device_id_type=MESH,
            ).start()

    to_plane(az, 2)

    @pl.when(at_end)
    def _():
        swap.wait()
        az_in[end] = az_swap[...]

    loads[5].wait()
    own_low, own_high = pairs_of(az_out, 0), pairs_of(az_out, 1)
    sounds = (ltab[0:1, :], ltab[1:2, :])
    used = azimuth_flux(own_high, own_low, *sounds)
    below = azimuth_flux(pairs_of(az_in, 0), own_low, *sounds)
    above = azimuth_flux(own_high, pairs_of(az_in, 1), *sounds)
    blank = jnp.zeros((2, ROWS), F32)
    weight = ltab[2:3, :]
    first = jnp.concatenate([weight * (a - b) for a, b in zip(below, used)] + [blank], axis=0)
    last = jnp.concatenate([weight * (b - a) for a, b in zip(above, used)] + [blank], axis=0)
    lane_id = lax.broadcasted_iota(jnp.int32, (ROWS, 128), 1)
    for at, lane, rim in ((0, 0, first.T), (CELLS - 128, 127, last.T)):
        for f in range(6):
            here = (f // 2, f % 2, slice(None), pl.ds(at, 128))
            delta = jnp.broadcast_to(rim[:, f : f + 1], (ROWS, 128))
            part[here] = part[here] + jnp.where(lane_id == lane, delta, 0.0)

    cross.wait_recv()
    to_plane(partner[0], 3)
    for n in (2, 3):
        whole(coef, 15)(recv_sem.at[n])
    cross.wait_send()
    for n in (0, 3, 4):
        whole(coef, 15)(send_sem.at[n])
    whole(coef.at[:, :, pl.ds(0, 128)], 15)(send_sem.at[1])


def finish(coef, part, fluid, tab, rtab, out_density, out_r, out_phi, out_pot, pot_buf, mom_buf, sem):
    first = pltpu.make_async_copy(part.at[0], out_density, sem.at[0])
    first.start()
    row_id = lax.broadcasted_iota(jnp.int32, (8, ROWS), 0)
    pots, forces = [], []
    for n in range(HALF):
        a, b = coef[n], coef[HALF + n]
        pots.append(jnp.where(row_id < 4, a, pltpu.roll(b, 4, 0)))
        forces.append(jnp.where(row_id < 4, pltpu.roll(a, 4, 0), b))

    def sides(tiles):
        value = jnp.concatenate(tiles, axis=0).T
        high = value.astype(BF16)
        return high, (value - high.astype(F32)).astype(BF16)

    def product(sides, table, rows):
        high, low = sides[0][rows], sides[1][rows]
        out = lax.dot_general(high, tab[table], NN, preferred_element_type=F32)
        out += lax.dot_general(low, tab[table], NN, preferred_element_type=F32)
        return out + lax.dot_general(high, tab[table + 1], NN, preferred_element_type=F32)

    pot, force = sides(pots), sides(forces)
    block = 64
    copies = []
    for n in range(ROWS // block):
        here = slice(n * block, (n + 1) * block)
        pot_buf[here, :] = product(pot, 0, here)
        radial = 0.1 * product(force, 0, here)
        azimuthal = product(pot, 2, here) * rtab[here, 9:10]
        inside = slice(8 + n * block, 8 + (n + 1) * block)
        for layer in range(LAYERS):
            rho = fluid[0, layer, inside, :]
            mom_buf[0, layer, here, :] = part[1, layer, here, :] + rho * radial
            mom_buf[1, layer, here, :] = part[2, layer, here, :] + rho * azimuthal
        for k, (src, dst) in enumerate(
            (
                (pot_buf.at[pl.ds(n * block, block), :], out_pot.at[pl.ds(n * block, block), :]),
                (mom_buf.at[0, :, pl.ds(n * block, block), :], out_r.at[:, pl.ds(n * block, block), :]),
                (mom_buf.at[1, :, pl.ds(n * block, block), :], out_phi.at[:, pl.ds(n * block, block), :]),
            )
        ):
            copy = pltpu.make_async_copy(src, dst, sem.at[1 + 3 * n + k])
            copy.start()
            copies.append(copy)
    first.wait()
    for copy in copies:
        copy.wait()


def local(density, mom_r, mom_phi, potential_kernel, force_kernel):
    tables = jnp.asarray(mode_tables())
    rows, lanes = (jnp.asarray(table) for table in row_tables())
    operands = (density, mom_r, mom_phi, potential_kernel, force_kernel, tables, rows, lanes)
    hbm = pl.BlockSpec(memory_space=pltpu.HBM)
    vmem = pl.BlockSpec(memory_space=pltpu.VMEM)
    dma = pltpu.SemaphoreType.DMA
    shared = (
        ((AZ, 8, ROWS), F32),
        ((3, LAYERS, ROWS, CELLS), F32),
        ((3, LAYERS, ROWS + 16, CELLS), F32),
        ((4, 128, CELLS), BF16),
        ((ROWS, 128), F32),
    )
    coef, part, fluid, tab, rtab = pl.pallas_call(
        exchange,
        out_shape=[pltpu.VMEM(shape, dtype) for shape, dtype in shared],
        in_specs=[hbm] * 8,
        out_specs=[vmem] * 5,
        scratch_shapes=[
            pltpu.VMEM((2, 2, ROWS, NR), BF16),
            pltpu.VMEM((8, ROWS), F32),
            pltpu.VMEM((2, ROWS, CELLS), BF16),
            pltpu.VMEM((HALF, 8, ROWS), F32),
            pltpu.VMEM((15, 8, ROWS), F32),
            pltpu.VMEM((2, 8, 128), F32),
            pltpu.VMEM((2, RAD, 8, 128), F32),
            pltpu.VMEM((2, 8, ROWS), F32),
            pltpu.VMEM((2, 8, ROWS), F32),
            pltpu.VMEM((8, ROWS), F32),
            pltpu.VMEM((2, 8, CELLS), F32),
            pltpu.VMEM((2, 8, CELLS), F32),
            pltpu.VMEM((3, LAYERS, 8, CELLS), F32),
            dma((8,)),
            dma((5,)),
            dma((4,)),
            dma((RAD,)),
            dma((5,)),
            dma((5,)),
        ],
        compiler_params=pltpu.CompilerParams(
            collective_id=0, has_side_effects=True, vmem_limit_bytes=32 * 2**20
        ),
        name="exchange",
    )(*(pltpu.with_memory_space_constraint(a, pltpu.HBM) for a in operands))
    fluid_shape = jax.ShapeDtypeStruct((LAYERS, ROWS, CELLS), F32)
    return pl.pallas_call(
        finish,
        out_shape=[fluid_shape, fluid_shape, fluid_shape, jax.ShapeDtypeStruct((ROWS, CELLS), F32)],
        in_specs=[vmem] * 5,
        out_specs=[hbm] * 4,
        scratch_shapes=[
            pltpu.VMEM((ROWS, CELLS), F32),
            pltpu.VMEM((2, LAYERS, ROWS, CELLS), F32),
            dma((1 + 3 * 4,)),
        ],
        compiler_params=pltpu.CompilerParams(vmem_limit_bytes=32 * 2**20),
        name="finish",
    )(coef, part, fluid, tab, rtab)


def solution(mesh):
    fluid = P(None, "rad", "az")
    kernel = P("az", "rad", None)
    return jax.shard_map(
        local,
        mesh=mesh,
        in_specs=(fluid, fluid, fluid, kernel, kernel),
        out_specs=(fluid, fluid, fluid, P("rad", "az")),
        check_vma=False,
    )
```

time: 38.2 us -> 34.8 us (0.911)
  Pallas kernels: 37.4 us -> 34.1 us
    pallas_call x1, Pallas kernels: 35.4 us -> 32.1 us  [local(): pl.pallas_call(exchange, out_shape=[pltpu.VMEM(shape, dtype) for shape, d...]
where the time goes in v2:
time: 34.8 us; the launch traced here: 34.7 us
  Pallas kernels  34.1 us (98%)
  between operations  0.64 us (2%)
    pallas_call x1, Pallas kernels, local(): pl.pallas_call(exchange, out_shape=[pltpu.VMEM(shape, dtype) for shape, d...  32.1 us
    pallas_call x1, Pallas kernels, local(): pl.pallas_call(finish, out_shape=[fluid_shape, fluid_shape, fluid_shape,...  1.96 us

profile of v2, /device:TPU:32, one launch (start us, length us, event | category | flops | bytes accessed | tf_op | source)
XLA Modules:
  0.0 34.7 jit_solution(14905499809638193822)
XLA Ops:
  0.6 32.1 %exchange.1 = (f32[32,8,256]{2,1,0:T(8,128)S(1)}, f32[3,2,256,512]{3,2,1,0:T(8,128)S(1)}, f32[3,2,272,512]{3,2,1,0:T(8,128)S(1)}, bf16[4,128,512]{2,1,0:T(8,128)(2,1)S(1)}, f32[256,128]{1,0:T(8,128)S(1)}) custom-call(f32[2,256,512]{2,1,0:T(8,128)} %density.1, f32[2,256,512]{2,1,0:T(8,128)} %mom_r.1, f32[2,256,512]{2,1,0:T(8,128)} %mom_phi.1, ...), custom_call_target="tpu_custom_call" | custom-call | tf_op jit(solution)/shard_map/exchange/pallas_call | solution.py:496
  32.8 2.0 %finish.1 = (f32[2,256,512]{2,1,0:T(8,128)}, f32[2,256,512]{2,1,0:T(8,128)}, f32[2,256,512]{2,1,0:T(8,128)}, f32[256,512]{1,0:T(8,128)}) custom-call(f32[32,8,256]{2,1,0:T(8,128)S(1)} %get-tuple-element.9.coef, f32[3,2,256,512]{3,2,1,0:T(8,128)S(1)} %get-tuple-element.10.part, f32[3,2,272,512]{3,2,1,0:T(8,128)S(1)} %get-tuple-element.11.fluid, ...), custom_call_target="tpu_custom_call" | custom-call | tf_op jit(solution)/shard_map/finish/pallas_call | solution.py:528

commit v3 on v2

--- a/solution.py
+++ b/solution.py
@@ -35,16 +35,17 @@
 
 def mode_tables():
     p, h, j = np.meshgrid(np.arange(16), np.arange(2), np.arange(4), indexing="ij")
-    column = (4 * (16 * h + p) + j).reshape(-1)
-    mode = (column // 2).astype(np.float64)
-    odd = (column % 2).astype(bool)
-    azimuth = (np.arange(NAZ) + 0.5) * STEP
-    angle = mode[:, None] * azimuth[None, :]
+    column = 4 * (16 * h + p) + j
+    mode = (column // 2).astype(np.float64)[..., None]
+    odd = (column % 2).astype(bool)[..., None]
+    angle = mode * ((np.arange(NAZ) + 0.5) * STEP)
     cos, sin = np.cos(angle), np.sin(angle)
-    basis = np.where(odd[:, None], sin, cos)
-    slope = np.where(odd[:, None], mode[:, None] * cos, -mode[:, None] * sin)
-    tables = np.stack([*split(basis), *split(slope)])
-    return np.ascontiguousarray(tables.reshape(4, 128, AZ, CELLS).transpose(2, 0, 1, 3))
+    basis = np.where(odd, sin, cos)
+    slope = np.where(odd, mode * cos, -mode * sin)
+    analysis = np.stack(split(basis)).reshape(2, 128, AZ, CELLS).transpose(2, 0, 1, 3)
+    synthesis = np.stack([split(basis), split(slope)]).transpose(0, 1, 3, 2, 4, 5)
+    synthesis = synthesis.reshape(2, 2, 2, 64, AZ, CELLS).transpose(4, 2, 0, 1, 3, 5)
+    return (np.ascontiguousarray(analysis), np.ascontiguousarray(synthesis))
 
 
 def row_tables():
@@ -120,20 +121,52 @@
     return [value[2 * c : 2 * c + 2] for c in range(3)]
 
 
+def stacked(tiles):
+    value = jnp.concatenate(tiles, axis=0)
+    high = value.astype(BF16).astype(F32)
+    return jnp.concatenate([high, high, value - high], axis=0).T.astype(BF16)
+
+
+def synthesis(coef, half, syn, sides):
+    row_id = lax.broadcasted_iota(jnp.int32, (8, ROWS), 0)
+    pots, forces = [], []
+    for n in range(0, HALF, 2):
+        a, b = coef[half * HALF + n], coef[half * HALF + n + 1]
+        pots.append(jnp.where(row_id < 4, a, pltpu.roll(b, 4, 0)))
+        forces.append(jnp.where(row_id < 4, pltpu.roll(a, 4, 0), b))
+    sides[0] = stacked(pots)
+    sides[1] = stacked(forces)
+
+    def product(here, side, table):
+        weights = syn[half, table].reshape(192, CELLS)
+        return lax.dot_general(sides[side, here, :], weights, NN, preferred_element_type=F32)
+
+    def at(here, rtab):
+        radial = 0.1 * product(here, 1, 0)
+        azimuthal = product(here, 0, 1) * rtab[here, 9:10]
+        return product(here, 0, 0), radial, azimuthal
+
+    return at
+
+
 def exchange(
     density,
     mom_r,
     mom_phi,
     pot_kernel,
     force_kernel,
+    analysis,
     tables,
     rows,
     lanes,
     coef,
     part,
     fluid,
+    syn,
+    rtab,
+    pot,
     tab,
-    rtab,
+    sides,
     kern,
     ltab,
     surf,
@@ -179,13 +212,15 @@
     inside = pl.ds(8, ROWS)
     loads = [
         pltpu.make_async_copy(density, fluid.at[0, :, inside, :], load_sem.at[0]),
-        pltpu.make_async_copy(tables.at[az], tab, load_sem.at[1]),
+        pltpu.make_async_copy(analysis.at[az], tab, load_sem.at[1]),
         pltpu.make_async_copy(mom_r, fluid.at[1, :, inside, :], load_sem.at[2]),
         pltpu.make_async_copy(mom_phi, fluid.at[2, :, inside, :], load_sem.at[3]),
         pltpu.make_async_copy(rows.at[pl.ds(rad * ROWS, ROWS), :], rtab, load_sem.at[4]),
         pltpu.make_async_copy(lanes.at[:, pl.ds(rad * ROWS, ROWS)], ltab, load_sem.at[5]),
         pltpu.make_async_copy(pot_kernel, kern.at[0], load_sem.at[6]),
         pltpu.make_async_copy(force_kernel, kern.at[1], load_sem.at[7]),
+        pltpu.make_async_copy(tables.at[az], syn.at[:, :, pl.ds(0, 2)], load_sem.at[8]),
+        pltpu.make_async_copy(tables.at[az, :, :, 0], syn.at[:, :, 2], load_sem.at[9]),
     ]
     for load in loads:
         load.start()
@@ -272,8 +307,7 @@
 
     size = 32
 
-    @pl.loop(0, ROWS // size)
-    def _(block):
+    def update(block):
         at = pl.multiple_of(block * size, size)
         here = pl.ds(at, size)
 
@@ -307,6 +341,9 @@
             for c in range(3):
                 part[c, layer, here, :] = new[c]
 
+    early = 4
+    pl.loop(0, early)(update)
+
     whole(arrived, 15)(recv_sem.at[0])
     total = chunks[p]
     for k in range(15):
@@ -325,6 +362,8 @@
             device_id_type=MESH,
         ).start()
 
+    pl.loop(early, ROWS // size)(update)
+
     edges[2].wait()
     edges[3].wait()
     for side, (outermost, sign, weight, sound) in enumerate(
@@ -375,6 +414,17 @@
         m = n % 2
         coef[az, 2 * n : 2 * n + 2, :] = products[n][2 * m : 2 * m + 2]
 
+    def to_plane(slot, n):
+        for to in plane:
+            pltpu.make_async_remote_copy(
+                src_ref=coef.at[slot],
+                dst_ref=coef.at[slot],
+                send_sem=send_sem.at[1 + n],
+                recv_sem=recv_sem.at[n],
+                device_id=(z_hi * HALF + to, rad),
+                device_id_type=MESH,
+            ).start()
+
     cross = pltpu.make_async_remote_copy(
         src_ref=coef.at[az],
         dst_ref=coef.at[az],
@@ -383,16 +433,24 @@
         device_id=partner,
         device_id_type=MESH,
     )
-    cross.start()
-
-    def to_plane(slot, n):
-        for to in plane:
+
+    direct = rad < RAD // 2
+    far_sends = direct & (z_hi == 1)
+    far_receives = direct & (z_hi == 0)
+
+    @pl.when(jnp.logical_not(far_sends))
+    def _():
+        cross.start()
+
+    @pl.when(far_sends)
+    def _():
+        for to in plane + [p]:
             pltpu.make_async_remote_copy(
-                src_ref=coef.at[slot],
-                dst_ref=coef.at[slot],
-                send_sem=send_sem.at[1 + n],
-                recv_sem=recv_sem.at[n],
-                device_id=(z_hi * HALF + to, rad),
+                src_ref=coef.at[az],
+                dst_ref=coef.at[az],
+                send_sem=send_sem.at[2],
+                recv_sem=recv_sem.at[3],
+                device_id=(to, rad),
                 device_id_type=MESH,
             ).start()
 
@@ -420,55 +478,71 @@
             delta = jnp.broadcast_to(rim[:, f : f + 1], (ROWS, 128))
             part[here] = part[here] + jnp.where(lane_id == lane, delta, 0.0)
 
-    cross.wait_recv()
-    to_plane(partner[0], 3)
-    for n in (2, 3):
-        whole(coef, 15)(recv_sem.at[n])
-    cross.wait_send()
-    for n in (0, 3, 4):
+    @pl.when(jnp.logical_not(far_receives))
+    def _():
+        cross.wait_recv()
+        to_plane(partner[0], 3)
+
+    whole(coef, 15)(recv_sem.at[2])
+    loads[8].wait()
+    loads[9].wait()
+    gravity = synthesis(coef, z_hi, syn, sides)
+    block = 32
+
+    @pl.loop(0, ROWS // block)
+    def _(n):
+        first_row = pl.multiple_of(n * block, block)
+        here = pl.ds(first_row, block)
+        potential, radial, azimuthal = gravity(here, rtab)
+        pot[here, :] = potential
+        for layer in range(LAYERS):
+            rho = fluid[0, layer, pl.ds(first_row + 8, block), :]
+            part[1, layer, here, :] = part[1, layer, here, :] + rho * radial
+            part[2, layer, here, :] = part[2, layer, here, :] + rho * azimuthal
+
+    @pl.when(far_receives)
+    def _():
+        whole(coef, 16)(recv_sem.at[3])
+
+    @pl.when(jnp.logical_not(far_receives))
+    def _():
+        whole(coef, 15)(recv_sem.at[3])
+        whole(coef, 15)(send_sem.at[4])
+
+    @pl.when(far_sends)
+    def _():
+        whole(coef, 16)(send_sem.at[2])
+
+    @pl.when(jnp.logical_not(far_sends))
+    def _():
+        cross.wait_send()
+
+    for n in (0, 3):
         whole(coef, 15)(send_sem.at[n])
     whole(coef.at[:, :, pl.ds(0, 128)], 15)(send_sem.at[1])
 
 
-def finish(coef, part, fluid, tab, rtab, out_density, out_r, out_phi, out_pot, pot_buf, mom_buf, sem):
+def finish(coef, part, fluid, syn, rtab, pot, out_density, out_r, out_phi, out_pot, sides, pot_buf, mom_buf, sem):
     first = pltpu.make_async_copy(part.at[0], out_density, sem.at[0])
     first.start()
-    row_id = lax.broadcasted_iota(jnp.int32, (8, ROWS), 0)
-    pots, forces = [], []
-    for n in range(HALF):
-        a, b = coef[n], coef[HALF + n]
-        pots.append(jnp.where(row_id < 4, a, pltpu.roll(b, 4, 0)))
-        forces.append(jnp.where(row_id < 4, pltpu.roll(a, 4, 0), b))
-
-    def sides(tiles):
-        value = jnp.concatenate(tiles, axis=0).T
-        high = value.astype(BF16)
-        return high, (value - high.astype(F32)).astype(BF16)
-
-    def product(sides, table, rows):
-        high, low = sides[0][rows], sides[1][rows]
-        out = lax.dot_general(high, tab[table], NN, preferred_element_type=F32)
-        out += lax.dot_general(low, tab[table], NN, preferred_element_type=F32)
-        return out + lax.dot_general(high, tab[table + 1], NN, preferred_element_type=F32)
-
-    pot, force = sides(pots), sides(forces)
+    gravity = synthesis(coef, 1 - lax.axis_index("az") // HALF, syn, sides)
     block = 64
     copies = []
     for n in range(ROWS // block):
         here = slice(n * block, (n + 1) * block)
-        pot_buf[here, :] = product(pot, 0, here)
-        radial = 0.1 * product(force, 0, here)
-        azimuthal = product(pot, 2, here) * rtab[here, 9:10]
+        potential, radial, azimuthal = gravity(here, rtab)
+        pot_buf[here, :] = pot[here, :] + potential
         inside = slice(8 + n * block, 8 + (n + 1) * block)
         for layer in range(LAYERS):
             rho = fluid[0, layer, inside, :]
             mom_buf[0, layer, here, :] = part[1, layer, here, :] + rho * radial
             mom_buf[1, layer, here, :] = part[2, layer, here, :] + rho * azimuthal
+        rows = pl.ds(n * block, block)
         for k, (src, dst) in enumerate(
             (
-                (pot_buf.at[pl.ds(n * block, block), :], out_pot.at[pl.ds(n * block, block), :]),
-                (mom_buf.at[0, :, pl.ds(n * block, block), :], out_r.at[:, pl.ds(n * block, block), :]),
-                (mom_buf.at[1, :, pl.ds(n * block, block), :], out_phi.at[:, pl.ds(n * block, block), :]),
+                (pot_buf.at[rows, :], out_pot.at[rows, :]),
+                (mom_buf.at[0, :, rows, :], out_r.at[:, rows, :]),
+                (mom_buf.at[1, :, rows, :], out_phi.at[:, rows, :]),
             )
         ):
             copy = pltpu.make_async_copy(src, dst, sem.at[1 + 3 * n + k])
@@ -480,9 +554,9 @@
 
 
 def local(density, mom_r, mom_phi, potential_kernel, force_kernel):
-    tables = jnp.asarray(mode_tables())
+    analysis, tables = (jnp.asarray(table) for table in mode_tables())
     rows, lanes = (jnp.asarray(table) for table in row_tables())
-    operands = (density, mom_r, mom_phi, potential_kernel, force_kernel, tables, rows, lanes)
+    operands = (density, mom_r, mom_phi, potential_kernel, force_kernel, analysis, tables, rows, lanes)
     hbm = pl.BlockSpec(memory_space=pltpu.HBM)
     vmem = pl.BlockSpec(memory_space=pltpu.VMEM)
     dma = pltpu.SemaphoreType.DMA
@@ -490,15 +564,18 @@
         ((AZ, 8, ROWS), F32),
         ((3, LAYERS, ROWS, CELLS), F32),
         ((3, LAYERS, ROWS + 16, CELLS), F32),
-        ((4, 128, CELLS), BF16),
+        ((2, 2, 3, 64, CELLS), BF16),
         ((ROWS, 128), F32),
+        ((ROWS, CELLS), F32),
     )
-    coef, part, fluid, tab, rtab = pl.pallas_call(
+    shared = pl.pallas_call(
         exchange,
         out_shape=[pltpu.VMEM(shape, dtype) for shape, dtype in shared],
-        in_specs=[hbm] * 8,
-        out_specs=[vmem] * 5,
+        in_specs=[hbm] * 9,
+        out_specs=[vmem] * 6,
         scratch_shapes=[
+            pltpu.VMEM((2, 128, CELLS), BF16),
+            pltpu.VMEM((2, ROWS, 192), BF16),
             pltpu.VMEM((2, 2, ROWS, NR), BF16),
             pltpu.VMEM((8, ROWS), F32),
             pltpu.VMEM((2, ROWS, CELLS), BF16),
@@ -512,7 +589,7 @@
             pltpu.VMEM((2, 8, CELLS), F32),
             pltpu.VMEM((2, 8, CELLS), F32),
             pltpu.VMEM((3, LAYERS, 8, CELLS), F32),
-            dma((8,)),
+            dma((10,)),
             dma((5,)),
             dma((4,)),
             dma((RAD,)),
@@ -528,16 +605,17 @@
     return pl.pallas_call(
         finish,
         out_shape=[fluid_shape, fluid_shape, fluid_shape, jax.ShapeDtypeStruct((ROWS, CELLS), F32)],
-        in_specs=[vmem] * 5,
+        in_specs=[vmem] * 6,
         out_specs=[hbm] * 4,
         scratch_shapes=[
+            pltpu.VMEM((2, ROWS, 192), BF16),
             pltpu.VMEM((ROWS, CELLS), F32),
             pltpu.VMEM((2, LAYERS, ROWS, CELLS), F32),
             dma((1 + 3 * 4,)),
         ],
         compiler_params=pltpu.CompilerParams(vmem_limit_bytes=32 * 2**20),
         name="finish",
-    )(coef, part, fluid, tab, rtab)
+    )(*shared)
 
 
 def solution(mesh):

time: 34.8 us -> 32.2 us (0.925)
  the two profiles are of different devices: /device:TPU:32 before, /device:TPU:64 now
where the time goes in v3:
time: 32.2 us; the launch traced here: 32.1 us
  Pallas kernels  31.4 us (98%)
  between operations  0.64 us (2%)
    pallas_call x1, Pallas kernels, local(): pl.pallas_call(exchange, out_shape=[pltpu.VMEM(shape, dtype) for shape, d...  29.5 us
    pallas_call x1, Pallas kernels, local(): pl.pallas_call(finish, out_shape=[fluid_shape, fluid_shape, fluid_shape,...  1.98 us

profile of v3, /device:TPU:64, one launch (start us, length us, event | category | flops | bytes accessed | tf_op | source)
XLA Modules:
  0.0 32.1 jit_solution(15412517963483819049)
XLA Ops:
  0.6 29.5 %exchange.1 = (f32[32,8,256]{2,1,0:T(8,128)S(1)}, f32[3,2,256,512]{3,2,1,0:T(8,128)S(1)}, f32[3,2,272,512]{3,2,1,0:T(8,128)S(1)}, bf16[2,2,3,64,512]{4,3,2,1,0:T...) custom-call(f32[2,256,512]{2,1,0:T(8,128)} %density.1, f32[2,256,512]{2,1,0:T(8,128)} %mom_r.1, ...), custom_call_target="tpu_custom_call" | custom-call | tf_op jit(solution)/shard_map/exchange/pallas_call | solution.py:571
  30.1 2.0 %finish.1 = (f32[2,256,512]{2,1,0:T(8,128)}, f32[2,256,512]{2,1,0:T(8,128)}, f32[2,256,512]{2,1,0:T(8,128)}, f32[256,512]{1,0:T(8,128)}) custom-call(f32[32,8,256]{2,1,0:T(8,128)S(1)} %get-tuple-element.10.coef, f32[3,2,256,512]{3,2,1,0:T(8,128)S(1)} %get-tuple-element.11.part, f32[3,2,272,512]{3,2,1,0:T(8,128)S(1)} %get-tuple-element.12.fluid, ...), custom_call_target="tpu_custom_call" | custom-call | tf_op jit(solution)/shard_map/finish/pallas_call | solution.py:605

commit v4 on v3

--- a/solution.py
+++ b/solution.py
@@ -414,17 +414,24 @@
         m = n % 2
         coef[az, 2 * n : 2 * n + 2, :] = products[n][2 * m : 2 * m + 2]
 
-    def to_plane(slot, n):
-        for to in plane:
+    def to_plane(half, slot, targets, sent, received):
+        for to in targets:
             pltpu.make_async_remote_copy(
                 src_ref=coef.at[slot],
                 dst_ref=coef.at[slot],
-                send_sem=send_sem.at[1 + n],
-                recv_sem=recv_sem.at[n],
-                device_id=(z_hi * HALF + to, rad),
+                send_sem=send_sem.at[sent],
+                recv_sem=recv_sem.at[received],
+                device_id=(half * HALF + to, rad),
                 device_id_type=MESH,
             ).start()
 
+    near_end = rad < RAD // 2
+    roles = (
+        ((z_hi == 1) & near_end, 11, 0),
+        ((z_hi == 1) & jnp.logical_not(near_end), 5, 0),
+        ((z_hi == 0) & near_end, 0, 11),
+        ((z_hi == 0) & jnp.logical_not(near_end), 0, 5),
+    )
     cross = pltpu.make_async_remote_copy(
         src_ref=coef.at[az],
         dst_ref=coef.at[az],
@@ -433,28 +440,14 @@
         device_id=partner,
         device_id_type=MESH,
     )
-
-    direct = rad < RAD // 2
-    far_sends = direct & (z_hi == 1)
-    far_receives = direct & (z_hi == 0)
-
-    @pl.when(jnp.logical_not(far_sends))
-    def _():
-        cross.start()
-
-    @pl.when(far_sends)
-    def _():
-        for to in plane + [p]:
-            pltpu.make_async_remote_copy(
-                src_ref=coef.at[az],
-                dst_ref=coef.at[az],
-                send_sem=send_sem.at[2],
-                recv_sem=recv_sem.at[3],
-                device_id=(to, rad),
-                device_id_type=MESH,
-            ).start()
-
-    to_plane(az, 2)
+    cross.start()
+    for role, direct, _ in roles:
+
+        @pl.when(role)
+        def _(targets=plane[:direct]):
+            to_plane(1 - z_hi, az, targets, 5, 3)
+
+    to_plane(z_hi, az, plane, 3, 2)
 
     @pl.when(at_end)
     def _():
@@ -478,10 +471,12 @@
             delta = jnp.broadcast_to(rim[:, f : f + 1], (ROWS, 128))
             part[here] = part[here] + jnp.where(lane_id == lane, delta, 0.0)
 
-    @pl.when(jnp.logical_not(far_receives))
-    def _():
-        cross.wait_recv()
-        to_plane(partner[0], 3)
+    cross.wait_recv()
+    for role, _, direct in roles:
+
+        @pl.when(role)
+        def _(targets=plane[direct:]):
+            to_plane(z_hi, partner[0], targets, 4, 3)
 
     whole(coef, 15)(recv_sem.at[2])
     loads[8].wait()
@@ -500,22 +495,16 @@
             part[1, layer, here, :] = part[1, layer, here, :] + rho * radial
             part[2, layer, here, :] = part[2, layer, here, :] + rho * azimuthal
 
-    @pl.when(far_receives)
-    def _():
-        whole(coef, 16)(recv_sem.at[3])
-
-    @pl.when(jnp.logical_not(far_receives))
-    def _():
-        whole(coef, 15)(recv_sem.at[3])
-        whole(coef, 15)(send_sem.at[4])
-
-    @pl.when(far_sends)
-    def _():
-        whole(coef, 16)(send_sem.at[2])
-
-    @pl.when(jnp.logical_not(far_sends))
-    def _():
-        cross.wait_send()
+    whole(coef, 15)(recv_sem.at[3])
+    cross.wait_send()
+    for role, sent, passed_by in roles:
+
+        @pl.when(role)
+        def _(sent=sent, handed_on=15 - passed_by):
+            if sent:
+                whole(coef, sent)(send_sem.at[5])
+            if handed_on:
+                whole(coef, handed_on)(send_sem.at[4])
 
     for n in (0, 3):
         whole(coef, 15)(send_sem.at[n])
@@ -590,7 +579,7 @@
             pltpu.VMEM((2, 8, CELLS), F32),
             pltpu.VMEM((3, LAYERS, 8, CELLS), F32),
             dma((10,)),
-            dma((5,)),
+            dma((6,)),
             dma((4,)),
             dma((RAD,)),
             dma((5,)),

time: 32.2 us -> 31.5 us (0.978)
  the two profiles are of different devices: /device:TPU:64 before, /device:TPU:32 now
where the time goes in v4:
time: 31.5 us; the launch traced here: 31.4 us
  Pallas kernels  30.8 us (98%)
  between operations  0.64 us (2%)
    pallas_call x1, Pallas kernels, local(): pl.pallas_call(exchange, out_shape=[pltpu.VMEM(shape, dtype) for shape, d...  28.8 us
    pallas_call x1, Pallas kernels, local(): pl.pallas_call(finish, out_shape=[fluid_shape, fluid_shape, fluid_shape,...  1.98 us

profile of v4, /device:TPU:32, one launch (start us, length us, event | category | flops | bytes accessed | tf_op | source)
XLA Modules:
  0.0 31.4 jit_solution(3660999387188175781)
XLA Ops:
  0.6 28.8 %exchange.1 = (f32[32,8,256]{2,1,0:T(8,128)S(1)}, f32[3,2,256,512]{3,2,1,0:T(8,128)S(1)}, f32[3,2,272,512]{3,2,1,0:T(8,128)S(1)}, bf16[2,2,3,64,512]{4,3,2,1,0:T...) custom-call(f32[2,256,512]{2,1,0:T(8,128)} %density.1, f32[2,256,512]{2,1,0:T(8,128)} %mom_r.1, ...), custom_call_target="tpu_custom_call" | custom-call | tf_op jit(solution)/shard_map/exchange/pallas_call | solution.py:560
  29.4 2.0 %finish.1 = (f32[2,256,512]{2,1,0:T(8,128)}, f32[2,256,512]{2,1,0:T(8,128)}, f32[2,256,512]{2,1,0:T(8,128)}, f32[256,512]{1,0:T(8,128)}) custom-call(f32[32,8,256]{2,1,0:T(8,128)S(1)} %get-tuple-element.10.coef, f32[3,2,256,512]{3,2,1,0:T(8,128)S(1)} %get-tuple-element.11.part, f32[3,2,272,512]{3,2,1,0:T(8,128)S(1)} %get-tuple-element.12.fluid, ...), custom_call_target="tpu_custom_call" | custom-call | tf_op jit(solution)/shard_map/finish/pallas_call | solution.py:594

commit v5 on v4

--- a/solution.py
+++ b/solution.py
@@ -169,7 +169,6 @@
     sides,
     kern,
     ltab,
-    surf,
     chunks,
     arrived,
     halfsum,
@@ -210,8 +209,9 @@
         pl.semaphore_signal(barrier, inc=1, device_id=(half * HALF + p, to), device_id_type=MESH)
 
     inside = pl.ds(8, ROWS)
+    halves = (pl.ds(0, CELLS // 2), pl.ds(CELLS // 2, CELLS // 2))
     loads = [
-        pltpu.make_async_copy(density, fluid.at[0, :, inside, :], load_sem.at[0]),
+        pltpu.make_async_copy(density.at[:, :, halves[0]], fluid.at[0, :, inside, halves[0]], load_sem.at[0]),
         pltpu.make_async_copy(analysis.at[az], tab, load_sem.at[1]),
         pltpu.make_async_copy(mom_r, fluid.at[1, :, inside, :], load_sem.at[2]),
         pltpu.make_async_copy(mom_phi, fluid.at[2, :, inside, :], load_sem.at[3]),
@@ -222,23 +222,26 @@
         pltpu.make_async_copy(tables.at[az], syn.at[:, :, pl.ds(0, 2)], load_sem.at[8]),
         pltpu.make_async_copy(tables.at[az, :, :, 0], syn.at[:, :, 2], load_sem.at[9]),
     ]
-    for load in loads:
+    second = pltpu.make_async_copy(
+        density.at[:, :, halves[1]], fluid.at[0, :, inside, halves[1]], load_sem.at[10]
+    )
+    for load in (loads[0], loads[1], second):
         load.start()
 
-    loads[0].wait()
-
-    @pl.loop(0, ROWS // 32)
-    def _(block):
-        at = pl.multiple_of(block * 32, 32)
-        value = fluid[0, 0, pl.ds(8 + at, 32), :] + fluid[0, 1, pl.ds(8 + at, 32), :]
+    share = jnp.zeros((128, ROWS), F32)
+    for load, cells in zip((loads[0], second), halves):
+        load.wait()
+        value = fluid[0, 0, inside, cells] + fluid[0, 1, inside, cells]
         high = value.astype(BF16)
-        surf[0, pl.ds(at, 32), :] = high
-        surf[1, pl.ds(at, 32), :] = (value - high.astype(F32)).astype(BF16)
-
-    loads[1].wait()
-    share = lax.dot_general(tab[0], surf[0], NT, preferred_element_type=F32)
-    share += lax.dot_general(tab[0], surf[1], NT, preferred_element_type=F32)
-    share += lax.dot_general(tab[1], surf[0], NT, preferred_element_type=F32)
+        low = (value - high.astype(F32)).astype(BF16)
+        if load is second:
+            for later in loads[2:]:
+                later.start()
+        else:
+            loads[1].wait()
+        share += lax.dot_general(tab[0, :, cells], high, NT, preferred_element_type=F32)
+        share += lax.dot_general(tab[0, :, cells], low, NT, preferred_element_type=F32)
+        share += lax.dot_general(tab[1, :, cells], high, NT, preferred_element_type=F32)
     chunks[...] = share.reshape(HALF, 8, ROWS)
 
     pl.semaphore_wait(barrier, len(plane) + len(column))
@@ -567,7 +570,6 @@
             pltpu.VMEM((2, ROWS, 192), BF16),
             pltpu.VMEM((2, 2, ROWS, NR), BF16),
             pltpu.VMEM((8, ROWS), F32),
-            pltpu.VMEM((2, ROWS, CELLS), BF16),
             pltpu.VMEM((HALF, 8, ROWS), F32),
             pltpu.VMEM((15, 8, ROWS), F32),
             pltpu.VMEM((2, 8, 128), F32),
@@ -578,7 +580,7 @@
             pltpu.VMEM((2, 8, CELLS), F32),
             pltpu.VMEM((2, 8, CELLS), F32),
             pltpu.VMEM((3, LAYERS, 8, CELLS), F32),
-            dma((10,)),
+            dma((11,)),
             dma((6,)),
             dma((4,)),
             dma((RAD,)),

time: 31.5 us -> 31.6 us (level)
  no operation moved by 1% of the time
where the time goes in v5:
time: 31.6 us; the launch traced here: 31.4 us
  Pallas kernels  30.8 us (97%)
  between operations  0.64 us (2%)
    pallas_call x1, Pallas kernels, local(): pl.pallas_call(exchange, out_shape=[pltpu.VMEM(shape, dtype) for shape, d...  28.8 us
    pallas_call x1, Pallas kernels, local(): pl.pallas_call(finish, out_shape=[fluid_shape, fluid_shape, fluid_shape,...  1.98 us

profile of v5, /device:TPU:32, one launch (start us, length us, event | category | flops | bytes accessed | tf_op | source)
XLA Modules:
  0.0 31.4 jit_solution(6585228087022773476)
XLA Ops:
  0.6 28.8 %exchange.1 = (f32[32,8,256]{2,1,0:T(8,128)S(1)}, f32[3,2,256,512]{3,2,1,0:T(8,128)S(1)}, f32[3,2,272,512]{3,2,1,0:T(8,128)S(1)}, bf16[2,2,3,64,512]{4,3,2,1,0:T...) custom-call(f32[2,256,512]{2,1,0:T(8,128)} %density.1, f32[2,256,512]{2,1,0:T(8,128)} %mom_r.1, ...), custom_call_target="tpu_custom_call" | custom-call | tf_op jit(solution)/shard_map/exchange/pallas_call | solution.py:563
  29.4 2.0 %finish.1 = (f32[2,256,512]{2,1,0:T(8,128)}, f32[2,256,512]{2,1,0:T(8,128)}, f32[2,256,512]{2,1,0:T(8,128)}, f32[256,512]{1,0:T(8,128)}) custom-call(f32[32,8,256]{2,1,0:T(8,128)S(1)} %get-tuple-element.10.coef, f32[3,2,256,512]{3,2,1,0:T(8,128)S(1)} %get-tuple-element.11.part, f32[3,2,272,512]{3,2,1,0:T(8,128)S(1)} %get-tuple-element.12.fluid, ...), custom_call_target="tpu_custom_call" | custom-call | tf_op jit(solution)/shard_map/finish/pallas_call | solution.py:596
